TPU v7x, 256 devices: a whole 4x4x8 slice. The times are simulated.
256 devices in a mesh: dom: 32 (over y, z), feat: 8 (over x, core).
Axes of the slice: x: 4, y: 4, z: 8, core: 2. Of those that a mesh axis runs over, the one named last changes fastest.
Arguments:
- feats: bfloat16 [128, 262144], P('feat', 'dom'), may hold values from -6 to 6
- tile_vals: bfloat16 [10240, 128, 128], P('dom'), may hold values from -0.1875 to 0.1875
- tile_dst: int32 [10240], P('dom'), may hold values from 0 to 63
- tile_src: int32 [10240], P('dom'), may hold values from 0 to 111
- tile_count: int32 [32], P('dom'), may hold values from 80 to 320, as said below
- send_rows: int32 [32, 32, 64], P('dom'), may hold values from 0 to 8191
- hub_ids: int32 [4096], P('dom'), may hold values from 0 to 8191, as said below
- w_self: bfloat16 [128, 128], P('feat'), may hold values from -0.5 to 0.5
- w_neigh: bfloat16 [128, 128], P('feat'), may hold values from -0.5 to 0.5
- bias: float32 [128], P('feat'), may hold values from -3 to 3
- cotangent: bfloat16 [128, 262144], P('feat', 'dom'), may hold values from -6 to 6
Outputs:
- activated: bfloat16 [128, 262144], P('feat', 'dom')
- grad_feats: bfloat16 [128, 262144], P('feat', 'dom')
- grad_w_self: float32 [128, 128], P('feat')
- grad_w_neigh: float32 [128, 128], P('feat')
- grad_bias: float32 [128], P('feat')
Inputs may be any that keep to these rules, and one draw needn't show every extreme that they name: `tile_count`: the live tiles of a partition are its first ones; some partition has all 320 slots live. `hub_ids`: the 128 entries of one partition are distinct rows of that partition.
All inputs are finite; a program needn't handle non-finite values.
Results may differ from a plain program's by a relative error of at most 0.0075.
Values may be sent and summed in bfloat16 or wider, within the bound.
No kernel may reach another device: no remote copies, remote signals or barrier semaphores. Data moves between devices by JAX's collectives and lax.ppermute only.
A program may use at most 64 MiB of HBM per device.

v0:
```python
import functools
import math

import jax
import jax.numpy as jnp
from jax import lax
from jax.experimental import pallas as pl
from jax.experimental.pallas import tpu as pltpu
from jax.sharding import PartitionSpec as P

edge = 128
span = 256
group = 32
kept = 64
own_blocks = 64
stride = 8
sure = 2
bf16 = jnp.bfloat16
f32 = jnp.float32
vmem = pl.BlockSpec(memory_space=pltpu.VMEM)
smem = pl.BlockSpec(memory_space=pltpu.SMEM)
hbm = pl.BlockSpec(memory_space=pl.ANY)


def params(mib):
    return pltpu.CompilerParams(vmem_limit_bytes=mib * 1024 * 1024)


def far_off(*values):
    return [pltpu.with_memory_space_constraint(value, pltpu.HBM) for value in values]


def lanes(rows):
    return lax.broadcasted_iota(jnp.int32, (rows, edge), 1)


def split(values, pieces):
    parts = []
    for _ in range(pieces):
        part = values.astype(bf16)
        parts.append(part)
        values = values - part.astype(f32)
    return parts


def column_block(column):
    hi, mid, lo = split(column, 3)
    lane = lanes(column.shape[0])
    block = jnp.where(lane == 0, hi.astype(f32), 0.0)
    block = jnp.where(lane == 1, mid.astype(f32), block)
    return jnp.where(lane == 2, lo.astype(f32), block)


def pick_kernel(
    rows_ref, hub_ref, feats_ref, out_ref, index, near, hub, wide, blocks, picked, sems
):
    width, nodes = feats_ref.shape
    count = nodes // span
    pairs = rows_ref.shape[0] // 2
    half = edge // 2
    copies = [
        pltpu.make_async_copy(feats_ref, near, sems.at[0]),
        pltpu.make_async_copy(rows_ref, wide, sems.at[1]),
        pltpu.make_async_copy(hub_ref, hub, sems.at[2]),
    ]
    for copy in copies:
        copy.start()
    copies[1].wait()
    copies[2].wait()
    lane = lanes(1)
    for g in range(pairs):
        row = jnp.concatenate([wide[2 * g : 2 * g + 1, :], wide[2 * g + 1 : 2 * g + 2, :]], axis=1)
        index[g : g + 1, :] = row
    index[pairs : pairs + 1, :] = hub[...].reshape(1, edge)
    copies[0].wait()
    for b in range(count):
        blocks[b] = near[:, b * span : (b + 1) * span]
    sub = lax.broadcasted_iota(jnp.int32, (span, edge), 0)

    def step(g, carry):
        row = index[pl.ds(g, 1), :]
        home = jnp.broadcast_to(row >> 8, (width, edge))
        hot = jnp.where(sub == (row & (span - 1)), 1.0, 0.0).astype(bf16)
        found = jnp.dot(blocks[...].reshape(count * width, span), hot, preferred_element_type=f32)
        total = found[0:width]
        for b in range(1, count):
            total = jnp.where(home == b, found[b * width : (b + 1) * width], total)
        picked[g] = total
        return carry

    lax.fori_loop(0, pairs, step, 0, unroll=16)
    step(pairs, 0)
    lane = lanes(width)
    mine = picked[pairs].astype(bf16)
    for g in range(pairs):
        here = picked[g]
        turned = pltpu.roll(here, half, 1)
        for odd in range(2):
            first, second = (turned, here) if odd else (here, turned)
            out_ref[2 * g + odd, 0:width] = mine
            out_ref[2 * g + odd, width : 2 * width] = jnp.where(lane < half, first, second).astype(
                bf16
            )


def pick(rows, hub_ids, feats):
    width, nodes = feats.shape
    domains, slots = rows.shape
    groups = domains // 2 + 1
    return pl.pallas_call(
        pick_kernel,
        out_shape=(
            jax.ShapeDtypeStruct((domains, 2 * width, edge), bf16),
            jax.ShapeDtypeStruct((groups, edge), jnp.int32),
        ),
        in_specs=[hbm, hbm, hbm],
        out_specs=(vmem, vmem),
        scratch_shapes=[
            pltpu.VMEM((width, nodes), bf16),
            pltpu.VMEM((edge,), jnp.int32),
            pltpu.VMEM((domains, slots), jnp.int32),
            pltpu.VMEM((nodes // span, width, span), bf16),
            pltpu.VMEM((groups, width, edge), f32),
            pltpu.SemaphoreType.DMA((3,)),
        ],
        compiler_params=params(32),
        name="pick",
    )(*far_off(rows, hub_ids, feats))


def deal_kernel(feats_ref, cotangent_ref, self_ref, neigh_ref, bias_ref, *rest):
    peers = len(rest) - 4
    outs, (w_self, w_neigh, bias, sems) = rest[:peers], rest[peers:]
    width, nodes = feats_ref.shape
    share = nodes // peers
    here = lax.axis_index("feat")
    small = [
        pltpu.make_async_copy(self_ref, w_self, sems.at[0]),
        pltpu.make_async_copy(neigh_ref, w_neigh, sems.at[1]),
        pltpu.make_async_copy(bias_ref, bias, sems.at[2]),
    ]
    large = []
    for k, out in enumerate(outs):
        there = pl.ds(pl.multiple_of((here ^ k) * share, share), share)
        for place, ref in enumerate((feats_ref, cotangent_ref)):
            large.append(
                pltpu.make_async_copy(
                    ref.at[:, there],
                    out.at[:, place * share : (place + 1) * share],
                    sems.at[3 + 2 * k + place],
                )
            )
    for copy in small + large:
        copy.start()
    for copy in small:
        copy.wait()
    square = (width, width)
    diagonal = lax.broadcasted_iota(jnp.int32, square, 0) == lax.broadcasted_iota(
        jnp.int32, square, 1
    )
    spread_bias = jnp.broadcast_to(bias[...].reshape(1, width), square)
    column = jnp.sum(jnp.where(diagonal, spread_bias, 0.0), axis=1, keepdims=True)
    block = column_block(column).astype(bf16)
    for out in outs:
        out[:, 2 * share : 2 * share + edge] = w_self[...]
        out[:, 2 * share + edge : 2 * share + 2 * edge] = w_neigh[...]
        out[:, 2 * share + 2 * edge : 2 * share + 3 * edge] = block
    for copy in large:
        copy.wait()


def deal(feats, cotangent, w_self, w_neigh, bias, peers):
    width, nodes = feats.shape
    part = jax.ShapeDtypeStruct((width, 2 * nodes // peers + 3 * edge), bf16)
    return pl.pallas_call(
        deal_kernel,
        out_shape=(part,) * peers,
        in_specs=[hbm] * 5,
        out_specs=(vmem,) * peers,
        scratch_shapes=[
            pltpu.VMEM((width, edge), bf16),
            pltpu.VMEM((width, edge), bf16),
            pltpu.VMEM((width,), f32),
            pltpu.SemaphoreType.DMA((3 + 2 * peers,)),
        ],
        compiler_params=params(32),
        name="deal",
    )(*far_off(feats, cotangent, w_self, w_neigh, bias))


def products_of(lefts, tiles, turned):
    results = []
    for i in range(0, len(tiles), 2):
        left = jnp.concatenate([lefts[i], lefts[i + 1]], axis=0)
        right = jnp.concatenate([tiles[i], tiles[i + 1]], axis=0 if turned else 1)
        contract = (((1,), (1 if turned else 0,)), ((), ()))
        both = lax.dot_general(left, right, contract, preferred_element_type=f32)
        width = lefts[i].shape[0]
        results += [both[:width, :edge], both[width:, edge:]]
    return results


def walk_tiles(refs, scratch, prepare, table, total, turned):
    dst_ref, src_ref, count_ref, vals_ref = refs
    dst, src, count, held, sems, tile_sems = scratch
    spare = total.shape[0] - 1
    lists = [
        pltpu.make_async_copy(count_ref, count, sems.at[0]),
        pltpu.make_async_copy(dst_ref, dst, sems.at[1]),
        pltpu.make_async_copy(src_ref, src, sems.at[2]),
    ]

    def fetch(k):
        rows = pl.ds(k * group, group)
        return pltpu.make_async_copy(vals_ref.at[rows], held.at[rows], tile_sems.at[k])

    def begin(k, carry):
        fetch(k).start()
        return carry

    for copy in lists:
        copy.start()
    for k in range(sure):
        fetch(k).start()
    prepare()
    lists[0].wait()
    live = count[0]
    groups = (live + group - 1) // group
    lax.fori_loop(sure, groups, begin, 0)
    for copy in lists[1:]:
        copy.wait()

    def some(k, carry):
        first = k * group
        lefts, places = [], []
        for i in range(group):
            t = first + i
            target, source = dst[t], src[t]
            lefts.append(table[source if turned else target])
            places.append(jnp.where(t < live, target if turned else source, spare))
        fetch(k).wait()
        tiles = [held[first + i] for i in range(group)]
        for place, product in zip(places, products_of(lefts, tiles, turned)):
            total[place] += product
        return carry

    lax.fori_loop(0, groups, some, 0)


def tile_scratch(tiles):
    return [
        pltpu.SMEM((tiles,), jnp.int32),
        pltpu.SMEM((tiles,), jnp.int32),
        pltpu.SMEM((1,), jnp.int32),
        pltpu.VMEM((tiles, edge, edge), bf16),
        pltpu.SemaphoreType.DMA((3,)),
        pltpu.SemaphoreType.DMA((tiles // group,)),
    ]


def gather_kernel(
    dst_ref, src_ref, count_ref, vals_ref, feats_ref, recv_ref, out_ref, near, table, total, sem, *scratch
):
    width, nodes = feats_ref.shape
    own = nodes // edge
    domains = recv_ref.shape[0]
    peers = out_ref.shape[0]
    features = pltpu.make_async_copy(feats_ref, near, sem)
    features.start()

    def prepare():
        lane = lanes(width)
        for g in range(domains // 2):
            table[own + g] = jnp.where(
                lane < edge // 2,
                recv_ref[2 * g, width : 2 * width].astype(f32),
                recv_ref[2 * g + 1, width : 2 * width].astype(f32),
            ).astype(bf16)
        for q in range(domains):
            table[own + domains // 2 + q] = recv_ref[q, 0:width]
        total[...] = jnp.zeros_like(total)
        features.wait()
        for b in range(own):
            table[b] = near[:, b * edge : (b + 1) * edge]

    walk_tiles((dst_ref, src_ref, count_ref, vals_ref), scratch, prepare, table, total, True)
    per = own // peers
    for b in range(own):
        col = (b % per) * edge
        out_ref[b // per, :, col : col + edge] = total[b].astype(bf16)


def gather(dst, src, count, vals, feats, recv, peers):
    width, nodes = feats.shape
    own = nodes // edge
    domains = recv.shape[0]
    return pl.pallas_call(
        gather_kernel,
        out_shape=jax.ShapeDtypeStruct((peers, width, nodes // peers), bf16),
        in_specs=[hbm] * 5 + [vmem],
        out_specs=vmem,
        scratch_shapes=[
            pltpu.VMEM((width, nodes), bf16),
            pltpu.VMEM((own + domains // 2 + domains, width, edge), bf16),
            pltpu.VMEM((own + 1, width, edge), f32),
            pltpu.SemaphoreType.DMA,
        ]
        + tile_scratch(vals.shape[0]),
        compiler_params=params(32),
        name="gather",
    )(*far_off(dst, src), count, *far_off(vals, feats), recv)


def list_kernel(
    dst_ref, src_ref, count_ref, vals_ref, work_ref, kept_ref, dst, src, count, work, sems, tile_sems
):
    copies = [
        pltpu.make_async_copy(count_ref, count, sems.at[0]),
        pltpu.make_async_copy(dst_ref, dst, sems.at[1]),
        pltpu.make_async_copy(src_ref, src, sems.at[2]),
    ]
    for copy in copies:
        copy.start()
    for copy in copies:
        copy.wait()
    tiles = dst.shape[0]
    live = count[0]

    def some(k, ends):
        low, high = ends
        for i in range(stride):
            t = k * stride + i
            source = src[t]
            alive, far = t < live, source >= own_blocks
            place = jnp.where(alive, jnp.where(far, high, low), tiles + 2)
            work[place] = t + (dst[t] << 9) + (source << 18)
            low = low + jnp.where(alive & ~far, 1, 0)
            high = high - jnp.where(alive & far, 1, 0)
        return low, high

    middle, _ = lax.fori_loop(0, (live + stride - 1) // stride, some, (0, live - 1))
    work[tiles] = middle
    work[tiles + 1] = live
    record = pltpu.make_async_copy(work, work_ref, sems.at[3])
    record.start()
    early = jnp.minimum(middle + kept, live)
    fetch(work, vals_ref, kept_ref, tile_sems, middle, early)

    def finish(k, carry):
        fetched(vals_ref, kept_ref, tile_sems, k)
        return carry

    lax.fori_loop(0, (early - middle + group - 1) // group, finish, 0)
    record.wait()


def list_tiles(dst, src, count, vals):
    tiles = dst.shape[0]
    part = jax.ShapeDtypeStruct((kept, edge, edge), bf16)
    return pl.pallas_call(
        list_kernel,
        out_shape=(jax.ShapeDtypeStruct((tiles + edge,), jnp.int32), part),
        in_specs=[hbm] * 4,
        out_specs=(vmem,) * 2,
        scratch_shapes=[
            pltpu.SMEM((tiles,), jnp.int32),
            pltpu.SMEM((tiles,), jnp.int32),
            pltpu.SMEM((1,), jnp.int32),
            pltpu.SMEM((tiles + edge,), jnp.int32),
            pltpu.SemaphoreType.DMA((4,)),
            pltpu.SemaphoreType.DMA((kept // group,)),
        ],
        compiler_params=params(16),
        name="list_tiles",
    )(*far_off(dst, src), count, *far_off(vals))


def fetch(work, vals_ref, held, sems, start, stop):
    def some(k, carry):
        for i in range(group):
            tile = work[jnp.minimum(start + k * group + i, stop - 1)] & 511
            pltpu.make_async_copy(vals_ref.at[tile], held.at[k * group + i], sems.at[k]).start()
        return carry

    lax.fori_loop(0, (stop - start + group - 1) // group, some, 0)


def fetched(vals_ref, held, sems, k):
    pltpu.make_async_copy(
        vals_ref.at[pl.ds(0, group)], held.at[pl.ds(k * group, group)], sems.at[k]
    ).wait()


def visit(work, held, ready, table, total, start, stop, turned):
    spare = total.shape[0] - 1

    def some(k, carry):
        slot = k * group
        first = start + slot
        lefts, tiles, places = [], [], []
        for i in range(group):
            code = work[jnp.minimum(first + i, stop - 1)]
            target = (code >> 9) & 511
            source = code >> 18
            lefts.append(table[source if turned else target])
            places.append(jnp.where(first + i < stop, target if turned else source, spare))
        ready(k)
        for i in range(group):
            tiles.append(held[slot + i])
        for place, product in zip(places, products_of(lefts, tiles, turned)):
            total[place] += product
        return carry

    lax.fori_loop(0, (stop - start + group - 1) // group, some, 0)


def fill_blocks(near_ref, blocks):
    own = blocks.shape[0]
    per = own // near_ref.shape[0]
    for b in range(own):
        col = (b % per) * edge
        blocks[b] = near_ref[b // per, :, col : col + edge]


def away_kernel(
    work, near_ref, kept_ref, vals_ref, out_ref, blocks, total, held, tile_sems
):
    peers, width, _ = near_ref.shape
    own = blocks.shape[0]
    share = own // peers * edge
    domains = out_ref.shape[0]
    far = own + domains // 2
    tiles = vals_ref.shape[0]
    middle, live = work[tiles], work[tiles + 1]
    early = jnp.minimum(middle + kept, live)
    fetch(work, vals_ref, held, tile_sems, early, live)
    fill_blocks(near_ref, blocks)
    total[...] = jnp.zeros_like(total)

    def summed(place):
        start = share + place * edge
        return jnp.sum(near_ref[:, :, start : start + edge].astype(f32), axis=0)

    grad_self = summed(0).astype(bf16)
    grad_neigh = summed(1).astype(bf16)
    grad_bias = column_block(jnp.sum(summed(2), axis=1, keepdims=True))
    grad_bias = pltpu.roll(grad_bias, edge // 2, 1)
    visit(work, kept_ref, lambda k: None, blocks, total, middle, early, False)
    ready = functools.partial(fetched, vals_ref, held, tile_sems)
    visit(work, held, ready, blocks, total, early, live, False)
    lane = lanes(width)
    for g in range(domains // 2):
        here = total[own + g]
        for odd in range(2):
            q = 2 * g + odd
            mine = pltpu.roll(here, edge // 2, 1) if odd else here
            out_ref[q, 0:width] = total[far + q].astype(bf16)
            out_ref[q, width : 2 * width] = jnp.where(lane < edge // 2, mine, grad_bias).astype(bf16)
            out_ref[q, 2 * width : 3 * width] = grad_self
            out_ref[q, 3 * width : 4 * width] = grad_neigh


def away(work, near, early, vals, domains, nodes):
    _, width, _ = near.shape
    tiles = vals.shape[0]
    own = nodes // edge
    return pl.pallas_call(
        away_kernel,
        out_shape=jax.ShapeDtypeStruct((domains, 4 * width, edge), bf16),
        in_specs=[smem, vmem, vmem, hbm],
        out_specs=vmem,
        scratch_shapes=[
            pltpu.VMEM((own, width, edge), bf16),
            pltpu.VMEM((own + domains // 2 + domains + 1, width, edge), f32),
            pltpu.VMEM((tiles, edge, edge), bf16),
            pltpu.SemaphoreType.DMA((tiles // group,)),
        ],
        compiler_params=params(32),
        name="away",
    )(work, near, early, *far_off(vals))


def home_kernel(work, near_ref, vals_ref, index, out_ref, hots, blocks, total, held, tile_sems):
    own = blocks.shape[0]
    tiles = vals_ref.shape[0]
    stop = work[tiles]
    fetch(work, vals_ref, held, tile_sems, 0, stop)
    fill_blocks(near_ref, blocks)
    total[...] = jnp.zeros_like(total)
    sub = lax.broadcasted_iota(jnp.int32, (span, edge), 0)
    groups = index.shape[0]
    for g in range(groups):
        hot = jnp.where(sub == (index[g : g + 1, :] & (span - 1)), 1.0, 0.0).astype(bf16)
        hots[:, g * edge : (g + 1) * edge] = hot
    for g in range(groups, groups + 2):
        hots[:, g * edge : (g + 1) * edge] = hot
    ready = functools.partial(fetched, vals_ref, held, tile_sems)
    visit(work, held, ready, blocks, total, 0, stop, False)
    for b in range(own):
        out_ref[:, b * edge : (b + 1) * edge] = total[b]


def home(work, near, vals, index, nodes):
    _, width, _ = near.shape
    tiles = vals.shape[0]
    own = nodes // edge
    return pl.pallas_call(
        home_kernel,
        out_shape=(
            jax.ShapeDtypeStruct((width, nodes), f32),
            jax.ShapeDtypeStruct((span, (index.shape[0] + 2) * edge), bf16),
        ),
        in_specs=[smem, vmem, hbm, vmem],
        out_specs=(vmem, vmem),
        scratch_shapes=[
            pltpu.VMEM((own, width, edge), bf16),
            pltpu.VMEM((own + 1, width, edge), f32),
            pltpu.VMEM((tiles, edge, edge), bf16),
            pltpu.SemaphoreType.DMA((tiles // group,)),
        ],
        compiler_params=params(32),
        name="home",
    )(work, near, *far_off(vals), index)


def layer_kernel(agg_ref, *rest):
    peers, width, share = agg_ref.shape
    rows = peers * width
    parts, near_ref, lates = rest[:peers], rest[peers], rest[peers + 1 : 2 * peers + 1]
    feats_all, cotangent_all, self_all, neigh_all, bias_all, act, back = rest[2 * peers + 1 :]
    here = lax.axis_index("feat")
    for k, part in enumerate(parts):
        peer = here ^ k
        feats_all[peer] = part[:, 0:share]
        cotangent_all[peer] = part[:, share : 2 * share]
        self_all[peer] = part[:, 2 * share : 2 * share + edge]
        neigh_all[peer] = part[:, 2 * share + edge : 2 * share + 2 * edge]
        bias_all[peer] = part[:, 2 * share + 2 * edge : 2 * share + 3 * edge]
    feats = feats_all[...].reshape(rows, share)
    cotangent = cotangent_all[...].reshape(rows, share)
    w_self = self_all[...].reshape(rows, edge)
    w_neigh = neigh_all[...].reshape(rows, edge)
    bias = jnp.sum(bias_all[...].reshape(rows, edge).astype(f32), axis=1, keepdims=True)
    aggregate = agg_ref[...].reshape(rows, share)
    first = (((0,), (0,)), ((), ()))
    last = (((1,), (1,)), ((), ()))
    linear = lax.dot_general(w_self, feats, first, preferred_element_type=f32)
    linear = linear + lax.dot_general(w_neigh, aggregate, first, preferred_element_type=f32)
    linear = linear + bias
    logistic = jax.nn.sigmoid(linear)
    act[...] = (linear * logistic).astype(bf16).reshape(peers, width, share)
    slope = logistic * (1.0 + linear * (1.0 - logistic))
    grad = (cotangent.astype(f32) * slope).astype(bf16)
    near_ref[:, :, 0:share] = (
        jnp.dot(w_neigh, grad, preferred_element_type=f32).astype(bf16).reshape(peers, width, share)
    )
    back[...] = (
        jnp.dot(w_self, grad, preferred_element_type=f32).astype(bf16).reshape(peers, width, share)
    )
    grad_self = lax.dot_general(feats, grad, last, preferred_element_type=f32)
    grad_neigh = lax.dot_general(aggregate, grad, last, preferred_element_type=f32)
    grad_bias = column_block(jnp.sum(grad.astype(f32), axis=1, keepdims=True)).astype(bf16)
    for place, piece in enumerate((grad_self.astype(bf16), grad_neigh.astype(bf16), grad_bias)):
        start = share + place * edge
        near_ref[:, :, start : start + edge] = piece.reshape(peers, width, edge)
    for k, late in enumerate(lates):
        peer = here ^ k
        late[:, 0:share] = act[peer]
        late[:, share : 2 * share] = back[peer]


def layer(agg, parts):
    peers, width, share = agg.shape
    return pl.pallas_call(
        layer_kernel,
        out_shape=(jax.ShapeDtypeStruct((peers, width, share + 3 * edge), bf16),)
        + (jax.ShapeDtypeStruct((width, 2 * share), bf16),) * peers,
        in_specs=[vmem] * (1 + peers),
        out_specs=(vmem,) * (1 + peers),
        scratch_shapes=[
            pltpu.VMEM((peers, width, share), bf16),
            pltpu.VMEM((peers, width, share), bf16),
            pltpu.VMEM((peers, width, edge), bf16),
            pltpu.VMEM((peers, width, edge), bf16),
            pltpu.VMEM((peers, width, edge), bf16),
            pltpu.VMEM((peers, width, share), bf16),
            pltpu.VMEM((peers, width, share), bf16),
        ],
        compiler_params=params(32),
        name="layer",
    )(agg, *parts)


def settle_kernel(scale, index, hots, recv_ref, base_ref, *rest):
    width, nodes = base_ref.shape
    lates, rest = rest[:-7], rest[-7:]
    act_ref, feats_ref, self_ref, neigh_ref, bias_ref, marked, back = rest
    domains = recv_ref.shape[0]
    peers = len(lates)
    share = nodes // peers
    count = nodes // span
    pairs = domains // 2
    here = lax.axis_index("feat")
    for k, late in enumerate(lates):
        peer = here ^ k
        act_ref[:, pl.ds(pl.multiple_of(peer * share, share), share)] = late[:, 0:share]
        back[:, pl.ds(pl.multiple_of(peer * share, share), share)] = late[:, share : 2 * share]
    lane = lanes(width)

    def over(start):
        return jnp.sum(recv_ref[:, start : start + width].astype(f32), axis=0)

    hub = over(0)
    self_ref[...] = over(2 * width) * scale
    neigh_ref[...] = over(3 * width) * scale
    tail = jnp.where(lane >= edge // 2, over(width), 0.0)
    column = jnp.broadcast_to(jnp.sum(tail, axis=1, keepdims=True) * scale, (width, edge))
    row = lax.broadcasted_iota(jnp.int32, (width, edge), 0)
    bias_ref[...] = jnp.sum(jnp.where(row == lane, column, 0.0), axis=0)[:width]
    hub_pieces = split(hub, 3)
    for g in range(pairs + 3):
        if g < pairs:
            first = recv_ref[2 * g, width : 2 * width].astype(f32)
            second = pltpu.roll(recv_ref[2 * g + 1, width : 2 * width].astype(f32), edge // 2, 1)
            value = jnp.where(lane < edge // 2, first, second)
        else:
            value = hub_pieces[g - pairs].astype(f32)
        at = min(g, pairs)
        where = jnp.broadcast_to(index[at : at + 1, :] >> 8, (width, edge))
        for b in range(count):
            marked[b * width : (b + 1) * width, g * edge : (g + 1) * edge] = jnp.where(
                where == b, value, 0.0
            ).astype(bf16)
    placed = lax.dot_general(
        marked[...], hots[...], (((1,), (1,)), ((), ())), preferred_element_type=f32
    )
    for b in range(count):
        cols = slice(b * span, (b + 1) * span)
        feats_ref[:, cols] = (
            back[:, cols].astype(f32) + base_ref[:, cols] + placed[b * width : (b + 1) * width]
        ).astype(bf16)


def settle(index, hots, recv, base, lates, scale):
    width, nodes = base.shape
    domains = recv.shape[0]
    terms = (domains // 2 + 3) * edge
    return pl.pallas_call(
        functools.partial(settle_kernel, scale),
        out_shape=(
            jax.ShapeDtypeStruct((width, nodes), bf16),
            jax.ShapeDtypeStruct((width, nodes), bf16),
            jax.ShapeDtypeStruct((width, edge), f32),
            jax.ShapeDtypeStruct((width, edge), f32),
            jax.ShapeDtypeStruct((width,), f32),
        ),
        in_specs=[vmem] * (4 + len(lates)),
        out_specs=(vmem,) * 5,
        scratch_shapes=[
            pltpu.VMEM((nodes // span * width, terms), bf16),
            pltpu.VMEM((width, nodes), bf16),
        ],
        compiler_params=params(32),
        name="settle",
    )(index, hots, recv, base, *lates)


def swap(values, axis):
    return lax.all_to_all(values, axis, split_axis=0, concat_axis=0, tiled=True)


def trade(parts, axis):
    peers = len(parts)
    return [
        part if k == 0 else lax.ppermute(part, axis, [(i, i ^ k) for i in range(peers)])
        for k, part in enumerate(parts)
    ]


def local(
    feats,
    tile_vals,
    tile_dst,
    tile_src,
    tile_count,
    send_rows,
    hub_ids,
    w_self,
    w_neigh,
    bias,
    cotangent,
):
    nodes = feats.shape[1]
    domains = lax.axis_size("dom")
    peers = lax.axis_size("feat")
    picked, index = pick(send_rows[0], hub_ids, feats)
    picked, bias = lax.optimization_barrier((picked, bias))
    recv = swap(picked, "dom")
    parts = trade(deal(feats, cotangent, w_self, w_neigh, bias, peers), "feat")
    agg = gather(tile_dst, tile_src, tile_count, tile_vals, feats, recv, peers)
    agg, parts = lax.optimization_barrier((agg, parts))
    agg = swap(agg, "feat")
    near, *lates = layer(agg, parts)
    near, count = lax.optimization_barrier((near, tile_count))
    near = swap(near, "feat")
    work, early = list_tiles(tile_dst, tile_src, count, tile_vals)
    back = away(work, near, early, tile_vals, domains, nodes)
    back, lates = lax.optimization_barrier((back, lates))
    back = swap(back, "dom")
    lates = trade(lates, "feat")
    base, hots = home(work, near, tile_vals, index, nodes)
    scale = 1.0 / math.sqrt(nodes * domains)
    return settle(index, hots, back, base, lates, scale)


def solution(mesh):
    placed = (
        P("feat", "dom"),
        P("dom", None, None),
        P("dom"),
        P("dom"),
        P("dom"),
        P("dom", None, None),
        P("dom"),
        P("feat", None),
        P("feat", None),
        P("feat"),
        P("feat", "dom"),
    )
    return jax.shard_map(
        local,
        mesh=mesh,
        in_specs=placed,
        out_specs=(P("feat", "dom"), P("feat", "dom"), P("feat", None), P("feat", None), P("feat")),
        check_vma=False,
    )
```

profile of v0, /device:TPU:32, one launch (start us, length us, event | category | flops | bytes accessed | tf_op | source)
XLA Modules:
  0.0 87.7 jit_solution(9155950264614971919)
XLA Ops:
  0.6 3.1 %pick.1 = (bf16[32,32,128]{2,1,0:T(8,128)(2,1)}, s32[17,128]{1,0:T(8,128)S(1)}) custom-call(s32[32,64]{1,0:T(8,128)} %bitcast.1, s32[128]{0:T(128)} %hub_ref.1, bf16[16,8192]{1,0:T(8,128)(2,1)} %feats_ref.5), custom_call_target="tpu_custom_call" | custom-call | tf_op jit(solution)/shard_map/pick/pallas_call | solution.py:110
  3.7 11.4 %all-to-all-start = ((bf16[32,32,128]{2,1,0:T(8,128)(2,1)}), bf16[32,32,128]{2,1,0:T(8,128)(2,1)S(1)}, u32[]{:S(2)}, u32[]{:S(2)}) async-start(bf16[32,32,128]{2,1,0:T(8,128)(2,1)} %get-tuple-element.52), calls=%async_computation | async-start | bytes 524288 | tf_op jit(solution)/shard_map/all_to_all | solution.py:669
  15.1 1.2 %deal.1 = (bf16[16,2432]{1,0:T(8,128)(2,1)S(1)}, bf16[16,2432]{1,0:T(8,128)(2,1)S(1)}, bf16[16,2432]{1,0:T(8,128)(2,1)S(1)}, bf16[16,2432]{1,0:T(8,128)(2,1)S(1)...) custom-call(bf16[16,8192]{1,0:T(8,128)(2,1)} %feats_ref.5, ...), custom_call_target="tpu_custom_call" | custom-call | tf_op jit(solution)/shard_map/deal/pallas_call | solution.py:175
  16.3 0.1 collective-permute-start
  16.4 1.6 %collective-permute-start.1 = (bf16[16,2432]{1,0:T(8,128)(2,1)S(1)}, bf16[16,2432]{1,0:T(8,128)(2,1)S(1)}, u32[]{:S(2)}, u32[]{:S(2)}) collective-permute-start(bf16[16,2432]{1,0:T(8,128)(2,1)S(1)} %get-tuple-element.56), channel_id=1, source_target_pairs={{0,2},{1,3},{2,0},{3,1},{4,6},{5,7},{6,4},{7,5},{8,10},{9,11},{10,... | collective-permute-start | bytes 233480 | tf_op jit(solution)/shard_map/ppermute | solution.py:675
  18.0 0.3 collective-permute-start.2
  18.3 3.0 %collective-permute-start.3 = (bf16[16,2432]{1,0:T(8,128)(2,1)S(1)}, bf16[16,2432]{1,0:T(8,128)(2,1)S(1)}, u32[]{:S(2)}, u32[]{:S(2)}) collective-permute-start(bf16[16,2432]{1,0:T(8,128)(2,1)S(1)} %get-tuple-element.58), channel_id=1, source_target_pairs={{0,4},{1,5},{2,6},{3,7},{4,0},{5,1},{6,2},{7,3},{8,12},{9,13},{10,... | collective-permute-start | bytes 233480 | tf_op jit(solution)/shard_map/ppermute | solution.py:675
  21.3 0.2 collective-permute-start.4
  21.5 0.0 collective-permute-done.rest_1_
  21.5 2.8 %collective-permute-start.5 = (bf16[16,2432]{1,0:T(8,128)(2,1)S(1)}, bf16[16,2432]{1,0:T(8,128)(2,1)S(1)}, u32[]{:S(2)}, u32[]{:S(2)}) collective-permute-start(bf16[16,2432]{1,0:T(8,128)(2,1)S(1)} %get-tuple-element.60), channel_id=1, source_target_pairs={{0,6},{1,7},{2,4},{3,5},{4,2},{5,3},{6,0},{7,1},{8,14},{9,15},{10,... | collective-permute-start | bytes 233480 | tf_op jit(solution)/shard_map/ppermute | solution.py:675
  24.3 0.0 collective-permute-done.1.rest_2_
  24.3 0.2 collective-permute-start.6
  25.2 2.2 %all-to-all-done.recv_ref = bf16[32,32,128]{2,1,0:T(8,128)(2,1)S(1)} async-done(((bf16[32,32,128]{2,1,0:T(8,128)(2,1)}), bf16[32,32,128]{2,1,0:T(8,128)(2,1)S(1)}, u32[]{:S(2)}, u32[]{:S(2)}) %all-to-all-start) | async-done | bytes 262176 | tf_op jit(solution)/shard_map/all_to_all | solution.py:669
  27.4 3.3 %gather.1 = bf16[8,16,1024]{2,1,0:T(8,128)(2,1)S(1)} custom-call(s32[320]{0:T(512)} %dst_ref.3, s32[320]{0:T(512)} %src_ref.3, s32[1]{0:T(128)S(6)} %copy.16.count_ref, bf16[320,128,128]{2,1,0:T(8,128)(2,1)} %vals_ref.7, bf16[16,8192]{1,0:T(8,128)(2,1)} %feats_ref.5, bf16[32,32,128]{2,1,0:T(8,128)(2,1)S(1)} %all-to-all-done.recv_ref), custom_call_target="tpu_custom_call" | custom-call | tf_op jit(solution)/shard_map/gather/pallas_call | solution.py:297
  30.7 0.0 collective-permute-done.2.rest_3_
  30.7 0.0 collective-permute-done.3.rest_4_
  30.7 0.0 collective-permute-done.4.rest_5_
  30.7 0.0 collective-permute-done.5.rest_6_
  30.7 1.0 %collective-permute-done.6.rest_7_ = bf16[16,2432]{1,0:T(8,128)(2,1)S(1)} collective-permute-done((bf16[16,2432]{1,0:T(8,128)(2,1)S(1)}, bf16[16,2432]{1,0:T(8,128)(2,1)S(1)}, u32[]{:S(2)}, u32[]{:S(2)}) %collective-permute-start.6) | collective-permute-done | bytes 77856 | tf_op jit(solution)/shard_map/ppermute | solution.py:675
  31.7 10.7 %all_to_all.20.agg_ref = bf16[8,16,1024]{2,1,0:T(8,128)(2,1)S(1)} all-to-all(bf16[8,16,1024]{2,1,0:T(8,128)(2,1)S(1)} %gather.1), channel_id=1, replica_groups=mesh['dom'=32,'feat'=8] {'feat'}, dimensions={0} | all-to-all | bytes 524288 | tf_op jit(solution)/shard_map/all_to_all | solution.py:669
  42.3 1.7 %layer.1 = (bf16[8,16,1408]{2,1,0:T(8,128)(2,1)}, bf16[16,2048]{1,0:T(8,128)(2,1)S(1)}, bf16[16,2048]{1,0:T(8,128)(2,1)S(1)}, bf16[16,2048]{1,0:T(8,128)(2,1)S(1...) custom-call(bf16[8,16,1024]{2,1,0:T(8,128)(2,1)S(1)} %all_to_all.20., ...), custom_call_target="tpu_custom_call" | custom-call | tf_op jit(solution)/shard_map/layer/pallas_call | solution.py:574
  44.0 3.4 %all-to-all-start.2 = ((bf16[8,16,1408]{2,1,0:T(8,128)(2,1)}), bf16[8,16,1408]{2,1,0:T(8,128)(2,1)S(1)}, u32[]{:S(2)}, u32[]{:S(2)}) async-start(bf16[8,16,1408]{2,1,0:T(8,128)(2,1)} %get-tuple-element.74), calls=%async_computation.2 | async-start | bytes 720896 | tf_op jit(solution)/shard_map/all_to_all | solution.py:669
  47.5 4.0 %list_tiles.1 = (s32[448]{0:T(512)S(1)}, bf16[64,128,128]{2,1,0:T(8,128)(2,1)S(1)}) custom-call(s32[320]{0:T(512)} %dst_ref.3, s32[320]{0:T(512)} %src_ref.3, s32[1]{0:T(128)S(6)} %copy.16.count_ref, bf16[320,128,128]{2,1,0:T(8,128)(2,1)} %vals_ref.7), custom_call_target="tpu_custom_call" | custom-call | tf_op jit(solution)/shard_map/list_tiles/pallas_call | solution.py:360
  51.5 4.5 %all-to-all-done.2.near_ref = bf16[8,16,1408]{2,1,0:T(8,128)(2,1)S(1)} async-done(((bf16[8,16,1408]{2,1,0:T(8,128)(2,1)}), bf16[8,16,1408]{2,1,0:T(8,128)(2,1)S(1)}, u32[]{:S(2)}, u32[]{:S(2)}) %all-to-all-start.2) | async-done | bytes 360480 | tf_op jit(solution)/shard_map/all_to_all | solution.py:669
  56.0 2.4 %away.1 = bf16[32,64,128]{2,1,0:T(8,128)(2,1)} custom-call(s32[448]{0:T(512)S(1)} %get-tuple-element.73.work, bf16[8,16,1408]{2,1,0:T(8,128)(2,1)S(1)} %all-to-all-done.2.near_ref, bf16[64,128,128]{2,1,0:T(8,128)(2,1)S(1)} %get-tuple-element.76.kept_ref, bf16[320,128,128]{2,1,0:T(8,128)(2,1)} %vals_ref.7), custom_call_target="tpu_custom_call" | custom-call | tf_op jit(solution)/shard_map/away/pallas_call | solution.py:467
  58.4 10.2 %all-to-all-start.3 = ((bf16[32,64,128]{2,1,0:T(8,128)(2,1)}), bf16[32,64,128]{2,1,0:T(8,128)(2,1)S(1)}, u32[]{:S(2)}, u32[]{:S(2)}) async-start(bf16[32,64,128]{2,1,0:T(8,128)(2,1)} %away.1), calls=%async_computation.3 | async-start | bytes 1048576 | tf_op jit(solution)/shard_map/all_to_all | solution.py:669
  68.6 0.1 collective-permute-start.7
  68.7 0.7 collective-permute-start.8
  69.3 1.2 %collective-permute-start.9 = (bf16[16,2048]{1,0:T(8,128)(2,1)S(1)}, bf16[16,2048]{1,0:T(8,128)(2,1)S(1)}, u32[]{:S(2)}, u32[]{:S(2)}) collective-permute-start(bf16[16,2048]{1,0:T(8,128)(2,1)S(1)} %get-tuple-element.90), channel_id=1, source_target_pairs={{0,3},{1,2},{2,1},{3,0},{4,7},{5,6},{6,5},{7,4},{8,11},{9,10},{10,... | collective-permute-start | bytes 196616 | tf_op jit(solution)/shard_map/ppermute | solution.py:675
  70.5 0.9 %collective-permute-start.10 = (bf16[16,2048]{1,0:T(8,128)(2,1)S(1)}, bf16[16,2048]{1,0:T(8,128)(2,1)S(1)}, u32[]{:S(2)}, u32[]{:S(2)}) collective-permute-start(bf16[16,2048]{1,0:T(8,128)(2,1)S(1)} %get-tuple-element.91), channel_id=1, source_target_pairs={{0,4},{1,5},{2,6},{3,7},{4,0},{5,1},{6,2},{7,3},{8,12},{9,13},{10,... | collective-permute-start | bytes 196616 | tf_op jit(solution)/shard_map/ppermute | solution.py:675
  71.4 2.3 %collective-permute-start.11 = (bf16[16,2048]{1,0:T(8,128)(2,1)S(1)}, bf16[16,2048]{1,0:T(8,128)(2,1)S(1)}, u32[]{:S(2)}, u32[]{:S(2)}) collective-permute-start(bf16[16,2048]{1,0:T(8,128)(2,1)S(1)} %get-tuple-element.92), channel_id=1, source_target_pairs={{0,5},{1,4},{2,7},{3,6},{4,1},{5,0},{6,3},{7,2},{8,13},{9,12},{10,... | collective-permute-start | bytes 196616 | tf_op jit(solution)/shard_map/ppermute | solution.py:675
  73.8 0.0 collective-permute-done.7.rest_1_
  73.8 1.2 %collective-permute-start.12 = (bf16[16,2048]{1,0:T(8,128)(2,1)S(1)}, bf16[16,2048]{1,0:T(8,128)(2,1)S(1)}, u32[]{:S(2)}, u32[]{:S(2)}) collective-permute-start(bf16[16,2048]{1,0:T(8,128)(2,1)S(1)} %get-tuple-element.93), channel_id=1, source_target_pairs={{0,6},{1,7},{2,4},{3,5},{4,2},{5,3},{6,0},{7,1},{8,14},{9,15},{10,... | collective-permute-start | bytes 196616 | tf_op jit(solution)/shard_map/ppermute | solution.py:675
  74.9 0.0 collective-permute-done.8.rest_2_
  74.9 1.8 %collective-permute-start.13 = (bf16[16,2048]{1,0:T(8,128)(2,1)S(1)}, bf16[16,2048]{1,0:T(8,128)(2,1)S(1)}, u32[]{:S(2)}, u32[]{:S(2)}) collective-permute-start(bf16[16,2048]{1,0:T(8,128)(2,1)S(1)} %get-tuple-element.94), channel_id=1, source_target_pairs={{0,7},{1,6},{2,5},{3,4},{4,3},{5,2},{6,1},{7,0},{8,15},{9,14},{10,... | collective-permute-start | bytes 196616 | tf_op jit(solution)/shard_map/ppermute | solution.py:675
  76.8 2.9 %home.1 = (f32[16,8192]{1,0:T(8,128)S(1)}, bf16[256,2432]{1,0:T(8,128)(2,1)S(1)}) custom-call(s32[448]{0:T(512)S(1)} %get-tuple-element.73.work, bf16[8,16,1408]{2,1,0:T(8,128)(2,1)S(1)} %all-to-all-done.2.near_ref, bf16[320,128,128]{2,1,0:T(8,128)(2,1)} %vals_ref.7, s32[17,128]{1,0:T(8,128)S(1)} %get-tuple-element.50.index), custom_call_target="tpu_custom_call" | custom-call | tf_op jit(solution)/shard_map/home/pallas_call | solution.py:507
  79.6 0.0 collective-permute-done.9.rest_3_
  79.6 0.0 collective-permute-done.10.rest_4_
  79.6 0.0 collective-permute-done.11.rest_5_
  79.7 0.1 collective-permute-done.12.rest_6_
  79.8 0.7 collective-permute-done.13.rest_7_
  80.5 5.5 %all-to-all-done.3.recv_ref = bf16[32,64,128]{2,1,0:T(8,128)(2,1)S(1)} async-done(((bf16[32,64,128]{2,1,0:T(8,128)(2,1)}), bf16[32,64,128]{2,1,0:T(8,128)(2,1)S(1)}, u32[]{:S(2)}, u32[]{:S(2)}) %all-to-all-start.3) | async-done | bytes 524320 | tf_op jit(solution)/shard_map/all_to_all | solution.py:669
  86.0 1.7 %settle.1 = (bf16[16,8192]{1,0:T(8,128)(2,1)}, bf16[16,8192]{1,0:T(8,128)(2,1)}, f32[16,128]{1,0:T(8,128)}, f32[16,128]{1,0:T(8,128)}, f32[16]{0:T(128)}) custom-call(s32[17,128]{1,0:T(8,128)S(1)} %get-tuple-element.50.index, bf16[256,2432]{1,0:T(8,128)(2,1)S(1)} %get-tuple-element.75.hots, bf16[32,64,128]{2,1,0:T(8,128)(2,1)S(1)} %all-to-all-done.3.recv_ref, ...), custom_call_target="tpu_custom_call" | custom-call | tf_op jit(solution)/shard_map/settle/pallas_call | solution.py:648
Async XLA Ops:
  3.7 23.7 %all-to-all-start = ((bf16[32,32,128]{2,1,0:T(8,128)(2,1)}), bf16[32,32,128]{2,1,0:T(8,128)(2,1)S(1)}, u32[]{:S(2)}, u32[]{:S(2)}) async-start(bf16[32,32,128]{2,1,0:T(8,128)(2,1)} %get-tuple-element.52), calls=%async_computation | async-start | bytes 524288 | tf_op jit(solution)/shard_map/all_to_all | solution.py:669
  16.3 5.2 %collective-permute-start = (bf16[16,2432]{1,0:T(8,128)(2,1)S(1)}, bf16[16,2432]{1,0:T(8,128)(2,1)S(1)}, u32[]{:S(2)}, u32[]{:S(2)}) collective-permute-start(bf16[16,2432]{1,0:T(8,128)(2,1)S(1)} %get-tuple-element.55), channel_id=1, source_target_pairs={{0,1},{1,0},{2,3},{3,2},{4,5},{5,4},{6,7},{7,6},{8,9},{9,8},{10,11... | collective-permute-start | bytes 233480 | tf_op jit(solution)/shard_map/ppermute | solution.py:675
  16.4 7.9 %collective-permute-start.1 = (bf16[16,2432]{1,0:T(8,128)(2,1)S(1)}, bf16[16,2432]{1,0:T(8,128)(2,1)S(1)}, u32[]{:S(2)}, u32[]{:S(2)}) collective-permute-start(bf16[16,2432]{1,0:T(8,128)(2,1)S(1)} %get-tuple-element.56), channel_id=1, source_target_pairs={{0,2},{1,3},{2,0},{3,1},{4,6},{5,7},{6,4},{7,5},{8,10},{9,11},{10,... | collective-permute-start | bytes 233480 | tf_op jit(solution)/shard_map/ppermute | solution.py:675
  18.0 12.7 %collective-permute-start.2 = (bf16[16,2432]{1,0:T(8,128)(2,1)S(1)}, bf16[16,2432]{1,0:T(8,128)(2,1)S(1)}, u32[]{:S(2)}, u32[]{:S(2)}) collective-permute-start(bf16[16,2432]{1,0:T(8,128)(2,1)S(1)} %get-tuple-element.57), channel_id=1, source_target_pairs={{0,3},{1,2},{2,1},{3,0},{4,7},{5,6},{6,5},{7,4},{8,11},{9,10},{10,... | collective-permute-start | bytes 233480 | tf_op jit(solution)/shard_map/ppermute | solution.py:675
  18.3 12.4 %collective-permute-start.3 = (bf16[16,2432]{1,0:T(8,128)(2,1)S(1)}, bf16[16,2432]{1,0:T(8,128)(2,1)S(1)}, u32[]{:S(2)}, u32[]{:S(2)}) collective-permute-start(bf16[16,2432]{1,0:T(8,128)(2,1)S(1)} %get-tuple-element.58), channel_id=1, source_target_pairs={{0,4},{1,5},{2,6},{3,7},{4,0},{5,1},{6,2},{7,3},{8,12},{9,13},{10,... | collective-permute-start | bytes 233480 | tf_op jit(solution)/shard_map/ppermute | solution.py:675
  21.3 9.4 %collective-permute-start.4 = (bf16[16,2432]{1,0:T(8,128)(2,1)S(1)}, bf16[16,2432]{1,0:T(8,128)(2,1)S(1)}, u32[]{:S(2)}, u32[]{:S(2)}) collective-permute-start(bf16[16,2432]{1,0:T(8,128)(2,1)S(1)} %get-tuple-element.59), channel_id=1, source_target_pairs={{0,5},{1,4},{2,7},{3,6},{4,1},{5,0},{6,3},{7,2},{8,13},{9,12},{10,... | collective-permute-start | bytes 233480 | tf_op jit(solution)/shard_map/ppermute | solution.py:675
  21.5 9.2 %collective-permute-start.5 = (bf16[16,2432]{1,0:T(8,128)(2,1)S(1)}, bf16[16,2432]{1,0:T(8,128)(2,1)S(1)}, u32[]{:S(2)}, u32[]{:S(2)}) collective-permute-start(bf16[16,2432]{1,0:T(8,128)(2,1)S(1)} %get-tuple-element.60), channel_id=1, source_target_pairs={{0,6},{1,7},{2,4},{3,5},{4,2},{5,3},{6,0},{7,1},{8,14},{9,15},{10,... | collective-permute-start | bytes 233480 | tf_op jit(solution)/shard_map/ppermute | solution.py:675
  24.3 7.4 %collective-permute-start.6 = (bf16[16,2432]{1,0:T(8,128)(2,1)S(1)}, bf16[16,2432]{1,0:T(8,128)(2,1)S(1)}, u32[]{:S(2)}, u32[]{:S(2)}) collective-permute-start(bf16[16,2432]{1,0:T(8,128)(2,1)S(1)} %get-tuple-element.61), channel_id=1, source_target_pairs={{0,7},{1,6},{2,5},{3,4},{4,3},{5,2},{6,1},{7,0},{8,15},{9,14},{10,... | collective-permute-start | bytes 233480 | tf_op jit(solution)/shard_map/ppermute | solution.py:675
  44.0 12.0 %all-to-all-start.2 = ((bf16[8,16,1408]{2,1,0:T(8,128)(2,1)}), bf16[8,16,1408]{2,1,0:T(8,128)(2,1)S(1)}, u32[]{:S(2)}, u32[]{:S(2)}) async-start(bf16[8,16,1408]{2,1,0:T(8,128)(2,1)} %get-tuple-element.74), calls=%async_computation.2 | async-start | bytes 720896 | tf_op jit(solution)/shard_map/all_to_all | solution.py:669
  58.4 27.6 %all-to-all-start.3 = ((bf16[32,64,128]{2,1,0:T(8,128)(2,1)}), bf16[32,64,128]{2,1,0:T(8,128)(2,1)S(1)}, u32[]{:S(2)}, u32[]{:S(2)}) async-start(bf16[32,64,128]{2,1,0:T(8,128)(2,1)} %away.1), calls=%async_computation.3 | async-start | bytes 1048576 | tf_op jit(solution)/shard_map/all_to_all | solution.py:669
  68.6 5.2 %collective-permute-start.7 = (bf16[16,2048]{1,0:T(8,128)(2,1)S(1)}, bf16[16,2048]{1,0:T(8,128)(2,1)S(1)}, u32[]{:S(2)}, u32[]{:S(2)}) collective-permute-start(bf16[16,2048]{1,0:T(8,128)(2,1)S(1)} %get-tuple-element.88), channel_id=1, source_target_pairs={{0,1},{1,0},{2,3},{3,2},{4,5},{5,4},{6,7},{7,6},{8,9},{9,8},{10,11... | collective-permute-start | bytes 196616 | tf_op jit(solution)/shard_map/ppermute | solution.py:675
  68.7 6.2 %collective-permute-start.8 = (bf16[16,2048]{1,0:T(8,128)(2,1)S(1)}, bf16[16,2048]{1,0:T(8,128)(2,1)S(1)}, u32[]{:S(2)}, u32[]{:S(2)}) collective-permute-start(bf16[16,2048]{1,0:T(8,128)(2,1)S(1)} %get-tuple-element.89), channel_id=1, source_target_pairs={{0,2},{1,3},{2,0},{3,1},{4,6},{5,7},{6,4},{7,5},{8,10},{9,11},{10,... | collective-permute-start | bytes 196616 | tf_op jit(solution)/shard_map/ppermute | solution.py:675
  69.3 10.3 %collective-permute-start.9 = (bf16[16,2048]{1,0:T(8,128)(2,1)S(1)}, bf16[16,2048]{1,0:T(8,128)(2,1)S(1)}, u32[]{:S(2)}, u32[]{:S(2)}) collective-permute-start(bf16[16,2048]{1,0:T(8,128)(2,1)S(1)} %get-tuple-element.90), channel_id=1, source_target_pairs={{0,3},{1,2},{2,1},{3,0},{4,7},{5,6},{6,5},{7,4},{8,11},{9,10},{10,... | collective-permute-start | bytes 196616 | tf_op jit(solution)/shard_map/ppermute | solution.py:675
  70.5 9.1 %collective-permute-start.10 = (bf16[16,2048]{1,0:T(8,128)(2,1)S(1)}, bf16[16,2048]{1,0:T(8,128)(2,1)S(1)}, u32[]{:S(2)}, u32[]{:S(2)}) collective-permute-start(bf16[16,2048]{1,0:T(8,128)(2,1)S(1)} %get-tuple-element.91), channel_id=1, source_target_pairs={{0,4},{1,5},{2,6},{3,7},{4,0},{5,1},{6,2},{7,3},{8,12},{9,13},{10,... | collective-permute-start | bytes 196616 | tf_op jit(solution)/shard_map/ppermute | solution.py:675
  71.4 8.2 %collective-permute-start.11 = (bf16[16,2048]{1,0:T(8,128)(2,1)S(1)}, bf16[16,2048]{1,0:T(8,128)(2,1)S(1)}, u32[]{:S(2)}, u32[]{:S(2)}) collective-permute-start(bf16[16,2048]{1,0:T(8,128)(2,1)S(1)} %get-tuple-element.92), channel_id=1, source_target_pairs={{0,5},{1,4},{2,7},{3,6},{4,1},{5,0},{6,3},{7,2},{8,13},{9,12},{10,... | collective-permute-start | bytes 196616 | tf_op jit(solution)/shard_map/ppermute | solution.py:675
  73.8 6.0 %collective-permute-start.12 = (bf16[16,2048]{1,0:T(8,128)(2,1)S(1)}, bf16[16,2048]{1,0:T(8,128)(2,1)S(1)}, u32[]{:S(2)}, u32[]{:S(2)}) collective-permute-start(bf16[16,2048]{1,0:T(8,128)(2,1)S(1)} %get-tuple-element.93), channel_id=1, source_target_pairs={{0,6},{1,7},{2,4},{3,5},{4,2},{5,3},{6,0},{7,1},{8,14},{9,15},{10,... | collective-permute-start | bytes 196616 | tf_op jit(solution)/shard_map/ppermute | solution.py:675
  74.9 5.5 %collective-permute-start.13 = (bf16[16,2048]{1,0:T(8,128)(2,1)S(1)}, bf16[16,2048]{1,0:T(8,128)(2,1)S(1)}, u32[]{:S(2)}, u32[]{:S(2)}) collective-permute-start(bf16[16,2048]{1,0:T(8,128)(2,1)S(1)} %get-tuple-element.94), channel_id=1, source_target_pairs={{0,7},{1,6},{2,5},{3,4},{4,3},{5,2},{6,1},{7,0},{8,15},{9,14},{10,... | collective-permute-start | bytes 196616 | tf_op jit(solution)/shard_map/ppermute | solution.py:675
where the time goes:
time: 88.7 us; the launch traced here: 87.7 us
  starting transfers between devices  41.4 us (47%)
  Pallas kernels  20.2 us (23%)
  waiting for transfers between devices  14.1 us (16%)
  blocking collectives  10.7 us (12%)
  between operations  1.44 us (2%)
    all_to_all x3, starting transfers between devices, swap(): return lax.all_to_all(values, axis, split_axis=0, concat_axis=0, tiled=True)  25 us
    ppermute x14, starting transfers between devices, trade(): lax.ppermute(part, axis, [(i, i ^ k) for i in range(peers)])  16.4 us
    all_to_all x3, waiting for transfers between devices, swap(): return lax.all_to_all(values, axis, split_axis=0, concat_axis=0, tiled=True)  12.3 us
    all_to_all x1, blocking collectives, swap(): return lax.all_to_all(values, axis, split_axis=0, concat_axis=0, tiled=True)  10.7 us
    pallas_call x1, Pallas kernels, list_tiles(): pl.pallas_call(list_kernel, out_shape=(jax.ShapeDtypeStruct((tiles + edge...  4.01 us
    pallas_call x1, Pallas kernels, gather(): pl.pallas_call(gather_kernel, out_shape=jax.ShapeDtypeStruct((peers, widt...  3.27 us
    pallas_call x1, Pallas kernels, pick(): pl.pallas_call(pick_kernel, out_shape=(jax.ShapeDtypeStruct((domains, 2 *...  3.09 us
    pallas_call x1, Pallas kernels, home(): pl.pallas_call(home_kernel, out_shape=(jax.ShapeDtypeStruct((width, nodes...  2.85 us
  transfers between devices with their start and end apart: 17, of which 6 were waited for; matrix products, arithmetic and copies ran while one was open for 0% of the time, Pallas kernels for 13%

commit v1 on v0

--- a/solution.py
+++ b/solution.py
@@ -11,9 +11,6 @@
 edge = 128
 span = 256
 group = 32
-kept = 64
-own_blocks = 64
-stride = 8
 sure = 2
 bf16 = jnp.bfloat16
 f32 = jnp.float32
@@ -51,45 +48,105 @@
     return jnp.where(lane == 2, lo.astype(f32), block)
 
 
+def start_all(pairs, sems):
+    copies = []
+    for place, (source, target) in enumerate(pairs):
+        copies.append(pltpu.make_async_copy(source, target, sems.at[place]))
+        copies[-1].start()
+    return copies
+
+
 def pick_kernel(
-    rows_ref, hub_ref, feats_ref, out_ref, index, near, hub, wide, blocks, picked, sems
+    rows_ref,
+    hub_ref,
+    feats_ref,
+    cotangent_ref,
+    self_ref,
+    neigh_ref,
+    bias_ref,
+    dst_ref,
+    src_ref,
+    count_ref,
+    out_ref,
+    index,
+    work_ref,
+    *rest,
 ):
+    parts, rest = rest[:-14], rest[-14:]
+    near, hub, wide, blocks, picked, w_self, w_neigh, bias, dst, src, count, work, sems, part_sems = rest
     width, nodes = feats_ref.shape
-    count = nodes // span
+    span_count = nodes // span
+    own = nodes // edge
     pairs = rows_ref.shape[0] // 2
+    peers = len(parts)
+    share = nodes // peers
     half = edge // 2
-    copies = [
-        pltpu.make_async_copy(feats_ref, near, sems.at[0]),
-        pltpu.make_async_copy(rows_ref, wide, sems.at[1]),
-        pltpu.make_async_copy(hub_ref, hub, sems.at[2]),
-    ]
-    for copy in copies:
-        copy.start()
-    copies[1].wait()
-    copies[2].wait()
-    lane = lanes(1)
+    tiles = dst.shape[0]
+    per_step = tiles // pairs
+    copies = start_all(
+        (
+            (count_ref, count),
+            (rows_ref, wide),
+            (hub_ref, hub),
+            (feats_ref, near),
+            (dst_ref, dst),
+            (src_ref, src),
+            (self_ref, w_self),
+            (neigh_ref, w_neigh),
+            (bias_ref, bias),
+        ),
+        sems,
+    )
+    here = lax.axis_index("feat")
+    moves = []
+    for k, part in enumerate(parts):
+        there = pl.ds(pl.multiple_of((here ^ k) * share, share), share)
+        moves.append((feats_ref.at[:, there], part.at[:, 0:share]))
+        moves.append((cotangent_ref.at[:, there], part.at[:, share : 2 * share]))
+    moves = start_all(moves, part_sems)
+    for copy in copies[:3]:
+        copy.wait()
     for g in range(pairs):
         row = jnp.concatenate([wide[2 * g : 2 * g + 1, :], wide[2 * g + 1 : 2 * g + 2, :]], axis=1)
         index[g : g + 1, :] = row
     index[pairs : pairs + 1, :] = hub[...].reshape(1, edge)
-    copies[0].wait()
-    for b in range(count):
+    for copy in copies[3:]:
+        copy.wait()
+    live = count[0]
+    for b in range(span_count):
         blocks[b] = near[:, b * span : (b + 1) * span]
     sub = lax.broadcasted_iota(jnp.int32, (span, edge), 0)
 
-    def step(g, carry):
+    def find(g):
         row = index[pl.ds(g, 1), :]
         home = jnp.broadcast_to(row >> 8, (width, edge))
         hot = jnp.where(sub == (row & (span - 1)), 1.0, 0.0).astype(bf16)
-        found = jnp.dot(blocks[...].reshape(count * width, span), hot, preferred_element_type=f32)
+        whole = blocks[...].reshape(span_count * width, span)
+        found = jnp.dot(whole, hot, preferred_element_type=f32)
         total = found[0:width]
-        for b in range(1, count):
+        for b in range(1, span_count):
             total = jnp.where(home == b, found[b * width : (b + 1) * width], total)
         picked[g] = total
-        return carry
-
-    lax.fori_loop(0, pairs, step, 0, unroll=16)
-    step(pairs, 0)
+
+    def step(g, ends):
+        low, high = ends
+        find(g)
+        for i in range(per_step):
+            t = g * per_step + i
+            source = src[t]
+            alive, far = t < live, source >= own
+            place = jnp.where(alive, jnp.where(far, high, low), tiles + 2)
+            work[place] = t + (dst[t] << 9) + (source << 18)
+            low = low + jnp.where(alive & ~far, 1, 0)
+            high = high - jnp.where(alive & far, 1, 0)
+        return low, high
+
+    middle, _ = lax.fori_loop(0, pairs, step, (0, live - 1), unroll=pairs)
+    work[tiles] = middle
+    work[tiles + 1] = live
+    record = pltpu.make_async_copy(work, work_ref, sems.at[9])
+    record.start()
+    find(pairs)
     lane = lanes(width)
     mine = picked[pairs].astype(bf16)
     for g in range(pairs):
@@ -101,91 +158,60 @@
             out_ref[2 * g + odd, width : 2 * width] = jnp.where(lane < half, first, second).astype(
                 bf16
             )
-
-
-def pick(rows, hub_ids, feats):
+    square = (width, width)
+    diagonal = lax.broadcasted_iota(jnp.int32, square, 0) == lax.broadcasted_iota(
+        jnp.int32, square, 1
+    )
+    spread_bias = jnp.broadcast_to(bias[...].reshape(1, width), square)
+    column = jnp.sum(jnp.where(diagonal, spread_bias, 0.0), axis=1, keepdims=True)
+    block = column_block(column).astype(bf16)
+    for part in parts:
+        part[:, 2 * share : 2 * share + edge] = w_self[...]
+        part[:, 2 * share + edge : 2 * share + 2 * edge] = w_neigh[...]
+        part[:, 2 * share + 2 * edge : 2 * share + 3 * edge] = block
+    for move in moves:
+        move.wait()
+    record.wait()
+
+
+def pick(rows, hub_ids, feats, cotangent, w_self, w_neigh, bias, dst, src, count, peers):
     width, nodes = feats.shape
     domains, slots = rows.shape
     groups = domains // 2 + 1
+    tiles = dst.shape[0]
+    part = jax.ShapeDtypeStruct((width, 2 * nodes // peers + 3 * edge), bf16)
     return pl.pallas_call(
         pick_kernel,
         out_shape=(
             jax.ShapeDtypeStruct((domains, 2 * width, edge), bf16),
             jax.ShapeDtypeStruct((groups, edge), jnp.int32),
-        ),
-        in_specs=[hbm, hbm, hbm],
-        out_specs=(vmem, vmem),
+            jax.ShapeDtypeStruct((tiles + edge,), jnp.int32),
+        )
+        + (part,) * peers,
+        in_specs=[hbm] * 10,
+        out_specs=(vmem,) * (3 + peers),
         scratch_shapes=[
             pltpu.VMEM((width, nodes), bf16),
             pltpu.VMEM((edge,), jnp.int32),
             pltpu.VMEM((domains, slots), jnp.int32),
             pltpu.VMEM((nodes // span, width, span), bf16),
             pltpu.VMEM((groups, width, edge), f32),
-            pltpu.SemaphoreType.DMA((3,)),
+            pltpu.VMEM((width, edge), bf16),
+            pltpu.VMEM((width, edge), bf16),
+            pltpu.VMEM((width,), f32),
+            pltpu.SMEM((tiles,), jnp.int32),
+            pltpu.SMEM((tiles,), jnp.int32),
+            pltpu.SMEM((1,), jnp.int32),
+            pltpu.SMEM((tiles + edge,), jnp.int32),
+            pltpu.SemaphoreType.DMA((10,)),
+            pltpu.SemaphoreType.DMA((2 * peers,)),
         ],
         compiler_params=params(32),
         name="pick",
-    )(*far_off(rows, hub_ids, feats))
-
-
-def deal_kernel(feats_ref, cotangent_ref, self_ref, neigh_ref, bias_ref, *rest):
-    peers = len(rest) - 4
-    outs, (w_self, w_neigh, bias, sems) = rest[:peers], rest[peers:]
-    width, nodes = feats_ref.shape
-    share = nodes // peers
-    here = lax.axis_index("feat")
-    small = [
-        pltpu.make_async_copy(self_ref, w_self, sems.at[0]),
-        pltpu.make_async_copy(neigh_ref, w_neigh, sems.at[1]),
-        pltpu.make_async_copy(bias_ref, bias, sems.at[2]),
-    ]
-    large = []
-    for k, out in enumerate(outs):
-        there = pl.ds(pl.multiple_of((here ^ k) * share, share), share)
-        for place, ref in enumerate((feats_ref, cotangent_ref)):
-            large.append(
-                pltpu.make_async_copy(
-                    ref.at[:, there],
-                    out.at[:, place * share : (place + 1) * share],
-                    sems.at[3 + 2 * k + place],
-                )
-            )
-    for copy in small + large:
-        copy.start()
-    for copy in small:
-        copy.wait()
-    square = (width, width)
-    diagonal = lax.broadcasted_iota(jnp.int32, square, 0) == lax.broadcasted_iota(
-        jnp.int32, square, 1
-    )
-    spread_bias = jnp.broadcast_to(bias[...].reshape(1, width), square)
-    column = jnp.sum(jnp.where(diagonal, spread_bias, 0.0), axis=1, keepdims=True)
-    block = column_block(column).astype(bf16)
-    for out in outs:
-        out[:, 2 * share : 2 * share + edge] = w_self[...]
-        out[:, 2 * share + edge : 2 * share + 2 * edge] = w_neigh[...]
-        out[:, 2 * share + 2 * edge : 2 * share + 3 * edge] = block
-    for copy in large:
-        copy.wait()
-
-
-def deal(feats, cotangent, w_self, w_neigh, bias, peers):
-    width, nodes = feats.shape
-    part = jax.ShapeDtypeStruct((width, 2 * nodes // peers + 3 * edge), bf16)
-    return pl.pallas_call(
-        deal_kernel,
-        out_shape=(part,) * peers,
-        in_specs=[hbm] * 5,
-        out_specs=(vmem,) * peers,
-        scratch_shapes=[
-            pltpu.VMEM((width, edge), bf16),
-            pltpu.VMEM((width, edge), bf16),
-            pltpu.VMEM((width,), f32),
-            pltpu.SemaphoreType.DMA((3 + 2 * peers,)),
-        ],
-        compiler_params=params(32),
-        name="deal",
-    )(*far_off(feats, cotangent, w_self, w_neigh, bias))
+    )(
+        *far_off(rows, hub_ids, feats, cotangent, w_self, w_neigh, bias, dst, src),
+        count,
+    )
 
 
 def products_of(lefts, tiles, turned):
@@ -311,70 +337,6 @@
     )(*far_off(dst, src), count, *far_off(vals, feats), recv)
 
 
-def list_kernel(
-    dst_ref, src_ref, count_ref, vals_ref, work_ref, kept_ref, dst, src, count, work, sems, tile_sems
-):
-    copies = [
-        pltpu.make_async_copy(count_ref, count, sems.at[0]),
-        pltpu.make_async_copy(dst_ref, dst, sems.at[1]),
-        pltpu.make_async_copy(src_ref, src, sems.at[2]),
-    ]
-    for copy in copies:
-        copy.start()
-    for copy in copies:
-        copy.wait()
-    tiles = dst.shape[0]
-    live = count[0]
-
-    def some(k, ends):
-        low, high = ends
-        for i in range(stride):
-            t = k * stride + i
-            source = src[t]
-            alive, far = t < live, source >= own_blocks
-            place = jnp.where(alive, jnp.where(far, high, low), tiles + 2)
-            work[place] = t + (dst[t] << 9) + (source << 18)
-            low = low + jnp.where(alive & ~far, 1, 0)
-            high = high - jnp.where(alive & far, 1, 0)
-        return low, high
-
-    middle, _ = lax.fori_loop(0, (live + stride - 1) // stride, some, (0, live - 1))
-    work[tiles] = middle
-    work[tiles + 1] = live
-    record = pltpu.make_async_copy(work, work_ref, sems.at[3])
-    record.start()
-    early = jnp.minimum(middle + kept, live)
-    fetch(work, vals_ref, kept_ref, tile_sems, middle, early)
-
-    def finish(k, carry):
-        fetched(vals_ref, kept_ref, tile_sems, k)
-        return carry
-
-    lax.fori_loop(0, (early - middle + group - 1) // group, finish, 0)
-    record.wait()
-
-
-def list_tiles(dst, src, count, vals):
-    tiles = dst.shape[0]
-    part = jax.ShapeDtypeStruct((kept, edge, edge), bf16)
-    return pl.pallas_call(
-        list_kernel,
-        out_shape=(jax.ShapeDtypeStruct((tiles + edge,), jnp.int32), part),
-        in_specs=[hbm] * 4,
-        out_specs=(vmem,) * 2,
-        scratch_shapes=[
-            pltpu.SMEM((tiles,), jnp.int32),
-            pltpu.SMEM((tiles,), jnp.int32),
-            pltpu.SMEM((1,), jnp.int32),
-            pltpu.SMEM((tiles + edge,), jnp.int32),
-            pltpu.SemaphoreType.DMA((4,)),
-            pltpu.SemaphoreType.DMA((kept // group,)),
-        ],
-        compiler_params=params(16),
-        name="list_tiles",
-    )(*far_off(dst, src), count, *far_off(vals))
-
-
 def fetch(work, vals_ref, held, sems, start, stop):
     def some(k, carry):
         for i in range(group):
@@ -423,7 +385,7 @@
 
 
 def away_kernel(
-    work, near_ref, kept_ref, vals_ref, out_ref, blocks, total, held, tile_sems
+    work, near_ref, vals_ref, out_ref, blocks, total, held, tile_sems
 ):
     peers, width, _ = near_ref.shape
     own = blocks.shape[0]
@@ -432,8 +394,7 @@
     far = own + domains // 2
     tiles = vals_ref.shape[0]
     middle, live = work[tiles], work[tiles + 1]
-    early = jnp.minimum(middle + kept, live)
-    fetch(work, vals_ref, held, tile_sems, early, live)
+    fetch(work, vals_ref, held, tile_sems, middle, live)
     fill_blocks(near_ref, blocks)
     total[...] = jnp.zeros_like(total)
 
@@ -445,9 +406,8 @@
     grad_neigh = summed(1).astype(bf16)
     grad_bias = column_block(jnp.sum(summed(2), axis=1, keepdims=True))
     grad_bias = pltpu.roll(grad_bias, edge // 2, 1)
-    visit(work, kept_ref, lambda k: None, blocks, total, middle, early, False)
     ready = functools.partial(fetched, vals_ref, held, tile_sems)
-    visit(work, held, ready, blocks, total, early, live, False)
+    visit(work, held, ready, blocks, total, middle, live, False)
     lane = lanes(width)
     for g in range(domains // 2):
         here = total[own + g]
@@ -460,14 +420,14 @@
             out_ref[q, 3 * width : 4 * width] = grad_neigh
 
 
-def away(work, near, early, vals, domains, nodes):
+def away(work, near, vals, domains, nodes):
     _, width, _ = near.shape
     tiles = vals.shape[0]
     own = nodes // edge
     return pl.pallas_call(
         away_kernel,
         out_shape=jax.ShapeDtypeStruct((domains, 4 * width, edge), bf16),
-        in_specs=[smem, vmem, vmem, hbm],
+        in_specs=[smem, vmem, hbm],
         out_specs=vmem,
         scratch_shapes=[
             pltpu.VMEM((own, width, edge), bf16),
@@ -477,7 +437,7 @@
         ],
         compiler_params=params(32),
         name="away",
-    )(work, near, early, *far_off(vals))
+    )(work, near, *far_off(vals))
 
 
 def home_kernel(work, near_ref, vals_ref, index, out_ref, hots, blocks, total, held, tile_sems):
@@ -693,18 +653,27 @@
     nodes = feats.shape[1]
     domains = lax.axis_size("dom")
     peers = lax.axis_size("feat")
-    picked, index = pick(send_rows[0], hub_ids, feats)
-    picked, bias = lax.optimization_barrier((picked, bias))
+    picked, index, work, *parts = pick(
+        send_rows[0],
+        hub_ids,
+        feats,
+        cotangent,
+        w_self,
+        w_neigh,
+        bias,
+        tile_dst,
+        tile_src,
+        tile_count,
+        peers,
+    )
     recv = swap(picked, "dom")
-    parts = trade(deal(feats, cotangent, w_self, w_neigh, bias, peers), "feat")
+    parts = trade(parts, "feat")
     agg = gather(tile_dst, tile_src, tile_count, tile_vals, feats, recv, peers)
     agg, parts = lax.optimization_barrier((agg, parts))
     agg = swap(agg, "feat")
     near, *lates = layer(agg, parts)
-    near, count = lax.optimization_barrier((near, tile_count))
     near = swap(near, "feat")
-    work, early = list_tiles(tile_dst, tile_src, count, tile_vals)
-    back = away(work, near, early, tile_vals, domains, nodes)
+    back = away(work, near, tile_vals, domains, nodes)
     back, lates = lax.optimization_barrier((back, lates))
     back = swap(back, "dom")
     lates = trade(lates, "feat")

time: 88.7 us -> 89.9 us (1.014)
  blocking collectives: 10.7 us -> 22.6 us
  starting transfers between devices: 41.4 us -> 36.1 us
  waiting for transfers between devices: 14.1 us -> 10.3 us
  Pallas kernels: 20.2 us -> 18.4 us
    all_to_all x1 -> x2, blocking collectives: 10.7 us -> 22.6 us  [swap(): return lax.all_to_all(values, axis, split_axis=0, concat_axis=0, tiled=True)]
    all_to_all x3 -> x2, starting transfers between devices: 25 us -> 19.8 us  [swap(): return lax.all_to_all(values, axis, split_axis=0, concat_axis=0, tiled=True)]
    pallas_call x2 -> x0, Pallas kernels: 5.23 us -> none  [the longest x1 4.01 us: list_tiles(): pl.pallas_call(list_kernel, out_shape=(jax.ShapeDtypeStruct((tiles + edge...]
    pallas_call x1, Pallas kernels: 3.09 us -> 5.74 us  [pick(): pl.pallas_call(pick_kernel, out_shape=(jax.ShapeDtypeStruct((domains, 2 *...]
    all_to_all x3 -> x2, waiting for transfers between devices: 12.3 us -> 9.68 us  [swap(): return lax.all_to_all(values, axis, split_axis=0, concat_axis=0, tiled=True)]
    pallas_call x1, Pallas kernels: 2.39 us -> 3.84 us  [away(): pl.pallas_call(away_kernel, out_shape=jax.ShapeDtypeStruct((domains, 4 *...]
    ppermute x14, waiting for transfers between devices: 1.81 us -> 0.66 us  [trade(): lax.ppermute(part, axis, [(i, i ^ k) for i in range(peers)])]
  transfers between devices with their start and end apart: 17 -> 16, of which waited for: 6 -> 3; matrix products, arithmetic and copies ran while one was open for 0% -> 0% of each run, Pallas kernels for 13% -> 7%
where the time goes in v1:
time: 89.9 us; the launch traced here: 88.9 us
  starting transfers between devices  36.1 us (40%)
  blocking collectives  22.6 us (25%)
  Pallas kernels  18.4 us (20%)
  waiting for transfers between devices  10.3 us (11%)
  between operations  1.43 us (2%)
    all_to_all x2, blocking collectives, swap(): return lax.all_to_all(values, axis, split_axis=0, concat_axis=0, tiled=True)  22.6 us
    all_to_all x2, starting transfers between devices, swap(): return lax.all_to_all(values, axis, split_axis=0, concat_axis=0, tiled=True)  19.8 us
    ppermute x14, starting transfers between devices, trade(): lax.ppermute(part, axis, [(i, i ^ k) for i in range(peers)])  16.4 us
    all_to_all x2, waiting for transfers between devices, swap(): return lax.all_to_all(values, axis, split_axis=0, concat_axis=0, tiled=True)  9.68 us
    pallas_call x1, Pallas kernels, pick(): pl.pallas_call(pick_kernel, out_shape=(jax.ShapeDtypeStruct((domains, 2 *...  5.74 us
    pallas_call x1, Pallas kernels, away(): pl.pallas_call(away_kernel, out_shape=jax.ShapeDtypeStruct((domains, 4 *...  3.84 us
    pallas_call x1, Pallas kernels, gather(): pl.pallas_call(gather_kernel, out_shape=jax.ShapeDtypeStruct((peers, widt...  3.26 us
    pallas_call x1, Pallas kernels, home(): pl.pallas_call(home_kernel, out_shape=(jax.ShapeDtypeStruct((width, nodes...  3.02 us
  transfers between devices with their start and end apart: 16, of which 3 were waited for; matrix products, arithmetic and copies ran while one was open for 0% of the time, Pallas kernels for 7%

profile of v1, /device:TPU:32, one launch (start us, length us, event | category | flops | bytes accessed | tf_op | source)
XLA Modules:
  0.0 88.9 jit_solution(10006945226842193406)
XLA Ops:
  1.3 5.7 %pick.1 = (bf16[32,32,128]{2,1,0:T(8,128)(2,1)}, s32[17,128]{1,0:T(8,128)S(1)}, s32[448]{0:T(512)S(1)}, bf16[16,2432]{1,0:T(8,128)(2,1)S(1)}, bf16[16,2432]{1,0:...) custom-call(s32[32,64]{1,0:T(8,128)} %bitcast.1, ...), custom_call_target="tpu_custom_call" | custom-call | tf_op jit(solution)/shard_map/pick/pallas_call | solution.py:183
  7.0 11.4 %all-to-all-start = ((bf16[32,32,128]{2,1,0:T(8,128)(2,1)}), bf16[32,32,128]{2,1,0:T(8,128)(2,1)S(1)}, u32[]{:S(2)}, u32[]{:S(2)}) async-start(bf16[32,32,128]{2,1,0:T(8,128)(2,1)} %get-tuple-element.47), calls=%async_computation | async-start | bytes 524288 | tf_op jit(solution)/shard_map/all_to_all | solution.py:629
  18.4 0.1 collective-permute-start
  18.5 1.6 %collective-permute-start.1 = (bf16[16,2432]{1,0:T(8,128)(2,1)S(1)}, bf16[16,2432]{1,0:T(8,128)(2,1)S(1)}, u32[]{:S(2)}, u32[]{:S(2)}) collective-permute-start(bf16[16,2432]{1,0:T(8,128)(2,1)S(1)} %get-tuple-element.50), channel_id=1, source_target_pairs={{0,2},{1,3},{2,0},{3,1},{4,6},{5,7},{6,4},{7,5},{8,10},{9,11},{10,... | collective-permute-start | bytes 233480 | tf_op jit(solution)/shard_map/ppermute | solution.py:635
  20.1 0.3 collective-permute-start.2
  20.4 3.0 %collective-permute-start.3 = (bf16[16,2432]{1,0:T(8,128)(2,1)S(1)}, bf16[16,2432]{1,0:T(8,128)(2,1)S(1)}, u32[]{:S(2)}, u32[]{:S(2)}) collective-permute-start(bf16[16,2432]{1,0:T(8,128)(2,1)S(1)} %get-tuple-element.52), channel_id=1, source_target_pairs={{0,4},{1,5},{2,6},{3,7},{4,0},{5,1},{6,2},{7,3},{8,12},{9,13},{10,... | collective-permute-start | bytes 233480 | tf_op jit(solution)/shard_map/ppermute | solution.py:635
  23.4 0.2 collective-permute-start.4
  23.6 0.0 collective-permute-done.rest_1_
  23.6 2.8 %collective-permute-start.5 = (bf16[16,2432]{1,0:T(8,128)(2,1)S(1)}, bf16[16,2432]{1,0:T(8,128)(2,1)S(1)}, u32[]{:S(2)}, u32[]{:S(2)}) collective-permute-start(bf16[16,2432]{1,0:T(8,128)(2,1)S(1)} %get-tuple-element.54), channel_id=1, source_target_pairs={{0,6},{1,7},{2,4},{3,5},{4,2},{5,3},{6,0},{7,1},{8,14},{9,15},{10,... | collective-permute-start | bytes 233480 | tf_op jit(solution)/shard_map/ppermute | solution.py:635
  26.3 0.0 collective-permute-done.1.rest_2_
  26.4 0.2 collective-permute-start.6
  26.6 4.1 %all-to-all-done.recv_ref = bf16[32,32,128]{2,1,0:T(8,128)(2,1)S(1)} async-done(((bf16[32,32,128]{2,1,0:T(8,128)(2,1)}), bf16[32,32,128]{2,1,0:T(8,128)(2,1)S(1)}, u32[]{:S(2)}, u32[]{:S(2)}) %all-to-all-start) | async-done | bytes 262176 | tf_op jit(solution)/shard_map/all_to_all | solution.py:629
  30.7 3.3 %gather.1 = bf16[8,16,1024]{2,1,0:T(8,128)(2,1)S(1)} custom-call(s32[320]{0:T(512)} %dst_ref.3, s32[320]{0:T(512)} %src_ref.3, s32[1]{0:T(128)S(6)} %copy.16.count_ref, bf16[320,128,128]{2,1,0:T(8,128)(2,1)} %vals_ref.5, bf16[16,8192]{1,0:T(8,128)(2,1)} %feats_ref.3, bf16[32,32,128]{2,1,0:T(8,128)(2,1)S(1)} %all-to-all-done.recv_ref), custom_call_target="tpu_custom_call" | custom-call | tf_op jit(solution)/shard_map/gather/pallas_call | solution.py:323
  34.0 0.0 collective-permute-done.2.rest_3_
  34.0 0.0 collective-permute-done.3.rest_4_
  34.0 0.0 collective-permute-done.4.rest_5_
  34.0 0.0 collective-permute-done.5.rest_6_
  34.0 0.0 collective-permute-done.6.rest_7_
  34.0 11.6 %all_to_all.20.agg_ref = bf16[8,16,1024]{2,1,0:T(8,128)(2,1)S(1)} all-to-all(bf16[8,16,1024]{2,1,0:T(8,128)(2,1)S(1)} %gather.1), channel_id=1, replica_groups=mesh['dom'=32,'feat'=8] {'feat'}, dimensions={0} | all-to-all | bytes 524288 | tf_op jit(solution)/shard_map/all_to_all | solution.py:629
  45.7 0.9 %layer.1 = (bf16[8,16,1408]{2,1,0:T(8,128)(2,1)S(1)}, bf16[16,2048]{1,0:T(8,128)(2,1)S(1)}, bf16[16,2048]{1,0:T(8,128)(2,1)S(1)}, bf16[16,2048]{1,0:T(8,128)(2,1...) custom-call(bf16[8,16,1024]{2,1,0:T(8,128)(2,1)S(1)} %all_to_all.20., ...), custom_call_target="tpu_custom_call" | custom-call | tf_op jit(solution)/shard_map/layer/pallas_call | solution.py:534
  46.5 11.0 %all_to_all.21.near_ref = bf16[8,16,1408]{2,1,0:T(8,128)(2,1)S(1)} all-to-all(bf16[8,16,1408]{2,1,0:T(8,128)(2,1)S(1)} %get-tuple-element.65), channel_id=1, replica_groups=mesh['dom'=32,'feat'=8] {'feat'}, dimensions={0} | all-to-all | bytes 720896 | tf_op jit(solution)/shard_map/all_to_all | solution.py:629
  57.5 3.8 %away.1 = bf16[32,64,128]{2,1,0:T(8,128)(2,1)} custom-call(s32[448]{0:T(512)S(1)} %get-tuple-element.46.work, bf16[8,16,1408]{2,1,0:T(8,128)(2,1)S(1)} %all_to_all.21.near_ref, bf16[320,128,128]{2,1,0:T(8,128)(2,1)} %vals_ref.5), custom_call_target="tpu_custom_call" | custom-call | tf_op jit(solution)/shard_map/away/pallas_call | solution.py:427
  61.4 8.4 %all-to-all-start.3 = ((bf16[32,64,128]{2,1,0:T(8,128)(2,1)}), bf16[32,64,128]{2,1,0:T(8,128)(2,1)S(1)}, u32[]{:S(2)}, u32[]{:S(2)}) async-start(bf16[32,64,128]{2,1,0:T(8,128)(2,1)} %away.1), calls=%async_computation.3 | async-start | bytes 1048576 | tf_op jit(solution)/shard_map/all_to_all | solution.py:629
  69.8 0.1 collective-permute-start.7
  69.9 0.7 collective-permute-start.8
  70.5 1.2 %collective-permute-start.9 = (bf16[16,2048]{1,0:T(8,128)(2,1)S(1)}, bf16[16,2048]{1,0:T(8,128)(2,1)S(1)}, u32[]{:S(2)}, u32[]{:S(2)}) collective-permute-start(bf16[16,2048]{1,0:T(8,128)(2,1)S(1)} %get-tuple-element.80), channel_id=1, source_target_pairs={{0,3},{1,2},{2,1},{3,0},{4,7},{5,6},{6,5},{7,4},{8,11},{9,10},{10,... | collective-permute-start | bytes 196616 | tf_op jit(solution)/shard_map/ppermute | solution.py:635
  71.8 0.9 %collective-permute-start.10 = (bf16[16,2048]{1,0:T(8,128)(2,1)S(1)}, bf16[16,2048]{1,0:T(8,128)(2,1)S(1)}, u32[]{:S(2)}, u32[]{:S(2)}) collective-permute-start(bf16[16,2048]{1,0:T(8,128)(2,1)S(1)} %get-tuple-element.81), channel_id=1, source_target_pairs={{0,4},{1,5},{2,6},{3,7},{4,0},{5,1},{6,2},{7,3},{8,12},{9,13},{10,... | collective-permute-start | bytes 196616 | tf_op jit(solution)/shard_map/ppermute | solution.py:635
  72.7 2.3 %collective-permute-start.11 = (bf16[16,2048]{1,0:T(8,128)(2,1)S(1)}, bf16[16,2048]{1,0:T(8,128)(2,1)S(1)}, u32[]{:S(2)}, u32[]{:S(2)}) collective-permute-start(bf16[16,2048]{1,0:T(8,128)(2,1)S(1)} %get-tuple-element.82), channel_id=1, source_target_pairs={{0,5},{1,4},{2,7},{3,6},{4,1},{5,0},{6,3},{7,2},{8,13},{9,12},{10,... | collective-permute-start | bytes 196616 | tf_op jit(solution)/shard_map/ppermute | solution.py:635
  75.0 0.0 collective-permute-done.7.rest_1_
  75.0 1.2 %collective-permute-start.12 = (bf16[16,2048]{1,0:T(8,128)(2,1)S(1)}, bf16[16,2048]{1,0:T(8,128)(2,1)S(1)}, u32[]{:S(2)}, u32[]{:S(2)}) collective-permute-start(bf16[16,2048]{1,0:T(8,128)(2,1)S(1)} %get-tuple-element.83), channel_id=1, source_target_pairs={{0,6},{1,7},{2,4},{3,5},{4,2},{5,3},{6,0},{7,1},{8,14},{9,15},{10,... | collective-permute-start | bytes 196616 | tf_op jit(solution)/shard_map/ppermute | solution.py:635
  76.1 0.0 collective-permute-done.8.rest_2_
  76.1 1.8 %collective-permute-start.13 = (bf16[16,2048]{1,0:T(8,128)(2,1)S(1)}, bf16[16,2048]{1,0:T(8,128)(2,1)S(1)}, u32[]{:S(2)}, u32[]{:S(2)}) collective-permute-start(bf16[16,2048]{1,0:T(8,128)(2,1)S(1)} %get-tuple-element.84), channel_id=1, source_target_pairs={{0,7},{1,6},{2,5},{3,4},{4,3},{5,2},{6,1},{7,0},{8,15},{9,14},{10,... | collective-permute-start | bytes 196616 | tf_op jit(solution)/shard_map/ppermute | solution.py:635
  78.0 3.0 %home.1 = (f32[16,8192]{1,0:T(8,128)S(1)}, bf16[256,2432]{1,0:T(8,128)(2,1)S(1)}) custom-call(s32[448]{0:T(512)S(1)} %get-tuple-element.46.work, bf16[8,16,1408]{2,1,0:T(8,128)(2,1)S(1)} %all_to_all.21.near_ref, bf16[320,128,128]{2,1,0:T(8,128)(2,1)} %vals_ref.5, s32[17,128]{1,0:T(8,128)S(1)} %get-tuple-element.45.index), custom_call_target="tpu_custom_call" | custom-call | tf_op jit(solution)/shard_map/home/pallas_call | solution.py:467
  81.0 0.0 collective-permute-done.9.rest_3_
  81.0 0.0 collective-permute-done.10.rest_4_
  81.0 0.0 collective-permute-done.11.rest_5_
  81.0 0.0 collective-permute-done.12.rest_6_
  81.0 0.6 collective-permute-done.13.rest_7_
  81.7 5.6 %all-to-all-done.3.recv_ref = bf16[32,64,128]{2,1,0:T(8,128)(2,1)S(1)} async-done(((bf16[32,64,128]{2,1,0:T(8,128)(2,1)}), bf16[32,64,128]{2,1,0:T(8,128)(2,1)S(1)}, u32[]{:S(2)}, u32[]{:S(2)}) %all-to-all-start.3) | async-done | bytes 524320 | tf_op jit(solution)/shard_map/all_to_all | solution.py:629
  87.3 1.7 %settle.1 = (bf16[16,8192]{1,0:T(8,128)(2,1)}, bf16[16,8192]{1,0:T(8,128)(2,1)}, f32[16,128]{1,0:T(8,128)}, f32[16,128]{1,0:T(8,128)}, f32[16]{0:T(128)}) custom-call(s32[17,128]{1,0:T(8,128)S(1)} %get-tuple-element.45.index, bf16[256,2432]{1,0:T(8,128)(2,1)S(1)} %get-tuple-element.66.hots, bf16[32,64,128]{2,1,0:T(8,128)(2,1)S(1)} %all-to-all-done.3.recv_ref, ...), custom_call_target="tpu_custom_call" | custom-call | tf_op jit(solution)/shard_map/settle/pallas_call | solution.py:608
Async XLA Ops:
  7.0 23.7 %all-to-all-start = ((bf16[32,32,128]{2,1,0:T(8,128)(2,1)}), bf16[32,32,128]{2,1,0:T(8,128)(2,1)S(1)}, u32[]{:S(2)}, u32[]{:S(2)}) async-start(bf16[32,32,128]{2,1,0:T(8,128)(2,1)} %get-tuple-element.47), calls=%async_computation | async-start | bytes 524288 | tf_op jit(solution)/shard_map/all_to_all | solution.py:629
  18.4 5.2 %collective-permute-start = (bf16[16,2432]{1,0:T(8,128)(2,1)S(1)}, bf16[16,2432]{1,0:T(8,128)(2,1)S(1)}, u32[]{:S(2)}, u32[]{:S(2)}) collective-permute-start(bf16[16,2432]{1,0:T(8,128)(2,1)S(1)} %get-tuple-element.49), channel_id=1, source_target_pairs={{0,1},{1,0},{2,3},{3,2},{4,5},{5,4},{6,7},{7,6},{8,9},{9,8},{10,11... | collective-permute-start | bytes 233480 | tf_op jit(solution)/shard_map/ppermute | solution.py:635
  18.5 7.9 %collective-permute-start.1 = (bf16[16,2432]{1,0:T(8,128)(2,1)S(1)}, bf16[16,2432]{1,0:T(8,128)(2,1)S(1)}, u32[]{:S(2)}, u32[]{:S(2)}) collective-permute-start(bf16[16,2432]{1,0:T(8,128)(2,1)S(1)} %get-tuple-element.50), channel_id=1, source_target_pairs={{0,2},{1,3},{2,0},{3,1},{4,6},{5,7},{6,4},{7,5},{8,10},{9,11},{10,... | collective-permute-start | bytes 233480 | tf_op jit(solution)/shard_map/ppermute | solution.py:635
  20.1 13.9 %collective-permute-start.2 = (bf16[16,2432]{1,0:T(8,128)(2,1)S(1)}, bf16[16,2432]{1,0:T(8,128)(2,1)S(1)}, u32[]{:S(2)}, u32[]{:S(2)}) collective-permute-start(bf16[16,2432]{1,0:T(8,128)(2,1)S(1)} %get-tuple-element.51), channel_id=1, source_target_pairs={{0,3},{1,2},{2,1},{3,0},{4,7},{5,6},{6,5},{7,4},{8,11},{9,10},{10,... | collective-permute-start | bytes 233480 | tf_op jit(solution)/shard_map/ppermute | solution.py:635
  20.4 13.6 %collective-permute-start.3 = (bf16[16,2432]{1,0:T(8,128)(2,1)S(1)}, bf16[16,2432]{1,0:T(8,128)(2,1)S(1)}, u32[]{:S(2)}, u32[]{:S(2)}) collective-permute-start(bf16[16,2432]{1,0:T(8,128)(2,1)S(1)} %get-tuple-element.52), channel_id=1, source_target_pairs={{0,4},{1,5},{2,6},{3,7},{4,0},{5,1},{6,2},{7,3},{8,12},{9,13},{10,... | collective-permute-start | bytes 233480 | tf_op jit(solution)/shard_map/ppermute | solution.py:635
  23.4 10.6 %collective-permute-start.4 = (bf16[16,2432]{1,0:T(8,128)(2,1)S(1)}, bf16[16,2432]{1,0:T(8,128)(2,1)S(1)}, u32[]{:S(2)}, u32[]{:S(2)}) collective-permute-start(bf16[16,2432]{1,0:T(8,128)(2,1)S(1)} %get-tuple-element.53), channel_id=1, source_target_pairs={{0,5},{1,4},{2,7},{3,6},{4,1},{5,0},{6,3},{7,2},{8,13},{9,12},{10,... | collective-permute-start | bytes 233480 | tf_op jit(solution)/shard_map/ppermute | solution.py:635
  23.6 10.4 %collective-permute-start.5 = (bf16[16,2432]{1,0:T(8,128)(2,1)S(1)}, bf16[16,2432]{1,0:T(8,128)(2,1)S(1)}, u32[]{:S(2)}, u32[]{:S(2)}) collective-permute-start(bf16[16,2432]{1,0:T(8,128)(2,1)S(1)} %get-tuple-element.54), channel_id=1, source_target_pairs={{0,6},{1,7},{2,4},{3,5},{4,2},{5,3},{6,0},{7,1},{8,14},{9,15},{10,... | collective-permute-start | bytes 233480 | tf_op jit(solution)/shard_map/ppermute | solution.py:635
  26.4 7.7 %collective-permute-start.6 = (bf16[16,2432]{1,0:T(8,128)(2,1)S(1)}, bf16[16,2432]{1,0:T(8,128)(2,1)S(1)}, u32[]{:S(2)}, u32[]{:S(2)}) collective-permute-start(bf16[16,2432]{1,0:T(8,128)(2,1)S(1)} %get-tuple-element.55), channel_id=1, source_target_pairs={{0,7},{1,6},{2,5},{3,4},{4,3},{5,2},{6,1},{7,0},{8,15},{9,14},{10,... | collective-permute-start | bytes 233480 | tf_op jit(solution)/shard_map/ppermute | solution.py:635
  61.4 25.9 %all-to-all-start.3 = ((bf16[32,64,128]{2,1,0:T(8,128)(2,1)}), bf16[32,64,128]{2,1,0:T(8,128)(2,1)S(1)}, u32[]{:S(2)}, u32[]{:S(2)}) async-start(bf16[32,64,128]{2,1,0:T(8,128)(2,1)} %away.1), calls=%async_computation.3 | async-start | bytes 1048576 | tf_op jit(solution)/shard_map/all_to_all | solution.py:629
  69.8 5.2 %collective-permute-start.7 = (bf16[16,2048]{1,0:T(8,128)(2,1)S(1)}, bf16[16,2048]{1,0:T(8,128)(2,1)S(1)}, u32[]{:S(2)}, u32[]{:S(2)}) collective-permute-start(bf16[16,2048]{1,0:T(8,128)(2,1)S(1)} %get-tuple-element.78), channel_id=1, source_target_pairs={{0,1},{1,0},{2,3},{3,2},{4,5},{5,4},{6,7},{7,6},{8,9},{9,8},{10,11... | collective-permute-start | bytes 196616 | tf_op jit(solution)/shard_map/ppermute | solution.py:635
  69.9 6.3 %collective-permute-start.8 = (bf16[16,2048]{1,0:T(8,128)(2,1)S(1)}, bf16[16,2048]{1,0:T(8,128)(2,1)S(1)}, u32[]{:S(2)}, u32[]{:S(2)}) collective-permute-start(bf16[16,2048]{1,0:T(8,128)(2,1)S(1)} %get-tuple-element.79), channel_id=1, source_target_pairs={{0,2},{1,3},{2,0},{3,1},{4,6},{5,7},{6,4},{7,5},{8,10},{9,11},{10,... | collective-permute-start | bytes 196616 | tf_op jit(solution)/shard_map/ppermute | solution.py:635
  70.5 10.5 %collective-permute-start.9 = (bf16[16,2048]{1,0:T(8,128)(2,1)S(1)}, bf16[16,2048]{1,0:T(8,128)(2,1)S(1)}, u32[]{:S(2)}, u32[]{:S(2)}) collective-permute-start(bf16[16,2048]{1,0:T(8,128)(2,1)S(1)} %get-tuple-element.80), channel_id=1, source_target_pairs={{0,3},{1,2},{2,1},{3,0},{4,7},{5,6},{6,5},{7,4},{8,11},{9,10},{10,... | collective-permute-start | bytes 196616 | tf_op jit(solution)/shard_map/ppermute | solution.py:635
  71.8 9.3 %collective-permute-start.10 = (bf16[16,2048]{1,0:T(8,128)(2,1)S(1)}, bf16[16,2048]{1,0:T(8,128)(2,1)S(1)}, u32[]{:S(2)}, u32[]{:S(2)}) collective-permute-start(bf16[16,2048]{1,0:T(8,128)(2,1)S(1)} %get-tuple-element.81), channel_id=1, source_target_pairs={{0,4},{1,5},{2,6},{3,7},{4,0},{5,1},{6,2},{7,3},{8,12},{9,13},{10,... | collective-permute-start | bytes 196616 | tf_op jit(solution)/shard_map/ppermute | solution.py:635
  72.7 8.4 %collective-permute-start.11 = (bf16[16,2048]{1,0:T(8,128)(2,1)S(1)}, bf16[16,2048]{1,0:T(8,128)(2,1)S(1)}, u32[]{:S(2)}, u32[]{:S(2)}) collective-permute-start(bf16[16,2048]{1,0:T(8,128)(2,1)S(1)} %get-tuple-element.82), channel_id=1, source_target_pairs={{0,5},{1,4},{2,7},{3,6},{4,1},{5,0},{6,3},{7,2},{8,13},{9,12},{10,... | collective-permute-start | bytes 196616 | tf_op jit(solution)/shard_map/ppermute | solution.py:635
  75.0 6.1 %collective-permute-start.12 = (bf16[16,2048]{1,0:T(8,128)(2,1)S(1)}, bf16[16,2048]{1,0:T(8,128)(2,1)S(1)}, u32[]{:S(2)}, u32[]{:S(2)}) collective-permute-start(bf16[16,2048]{1,0:T(8,128)(2,1)S(1)} %get-tuple-element.83), channel_id=1, source_target_pairs={{0,6},{1,7},{2,4},{3,5},{4,2},{5,3},{6,0},{7,1},{8,14},{9,15},{10,... | collective-permute-start | bytes 196616 | tf_op jit(solution)/shard_map/ppermute | solution.py:635
  76.1 5.5 %collective-permute-start.13 = (bf16[16,2048]{1,0:T(8,128)(2,1)S(1)}, bf16[16,2048]{1,0:T(8,128)(2,1)S(1)}, u32[]{:S(2)}, u32[]{:S(2)}) collective-permute-start(bf16[16,2048]{1,0:T(8,128)(2,1)S(1)} %get-tuple-element.84), channel_id=1, source_target_pairs={{0,7},{1,6},{2,5},{3,4},{4,3},{5,2},{6,1},{7,0},{8,15},{9,14},{10,... | collective-permute-start | bytes 196616 | tf_op jit(solution)/shard_map/ppermute | solution.py:635

commit v2 on v1

--- a/solution.py
+++ b/solution.py
@@ -64,33 +64,23 @@
     self_ref,
     neigh_ref,
     bias_ref,
-    dst_ref,
-    src_ref,
-    count_ref,
     out_ref,
     index,
-    work_ref,
     *rest,
 ):
-    parts, rest = rest[:-14], rest[-14:]
-    near, hub, wide, blocks, picked, w_self, w_neigh, bias, dst, src, count, work, sems, part_sems = rest
+    parts, rest = rest[:-10], rest[-10:]
+    near, hub, wide, blocks, picked, w_self, w_neigh, bias, sems, part_sems = rest
     width, nodes = feats_ref.shape
     span_count = nodes // span
-    own = nodes // edge
     pairs = rows_ref.shape[0] // 2
     peers = len(parts)
     share = nodes // peers
     half = edge // 2
-    tiles = dst.shape[0]
-    per_step = tiles // pairs
     copies = start_all(
         (
-            (count_ref, count),
             (rows_ref, wide),
             (hub_ref, hub),
             (feats_ref, near),
-            (dst_ref, dst),
-            (src_ref, src),
             (self_ref, w_self),
             (neigh_ref, w_neigh),
             (bias_ref, bias),
@@ -104,20 +94,19 @@
         moves.append((feats_ref.at[:, there], part.at[:, 0:share]))
         moves.append((cotangent_ref.at[:, there], part.at[:, share : 2 * share]))
     moves = start_all(moves, part_sems)
-    for copy in copies[:3]:
+    for copy in copies[:2]:
         copy.wait()
     for g in range(pairs):
         row = jnp.concatenate([wide[2 * g : 2 * g + 1, :], wide[2 * g + 1 : 2 * g + 2, :]], axis=1)
         index[g : g + 1, :] = row
     index[pairs : pairs + 1, :] = hub[...].reshape(1, edge)
-    for copy in copies[3:]:
+    for copy in copies[2:]:
         copy.wait()
-    live = count[0]
     for b in range(span_count):
         blocks[b] = near[:, b * span : (b + 1) * span]
     sub = lax.broadcasted_iota(jnp.int32, (span, edge), 0)
 
-    def find(g):
+    def find(g, carry):
         row = index[pl.ds(g, 1), :]
         home = jnp.broadcast_to(row >> 8, (width, edge))
         hot = jnp.where(sub == (row & (span - 1)), 1.0, 0.0).astype(bf16)
@@ -127,26 +116,10 @@
         for b in range(1, span_count):
             total = jnp.where(home == b, found[b * width : (b + 1) * width], total)
         picked[g] = total
-
-    def step(g, ends):
-        low, high = ends
-        find(g)
-        for i in range(per_step):
-            t = g * per_step + i
-            source = src[t]
-            alive, far = t < live, source >= own
-            place = jnp.where(alive, jnp.where(far, high, low), tiles + 2)
-            work[place] = t + (dst[t] << 9) + (source << 18)
-            low = low + jnp.where(alive & ~far, 1, 0)
-            high = high - jnp.where(alive & far, 1, 0)
-        return low, high
-
-    middle, _ = lax.fori_loop(0, pairs, step, (0, live - 1), unroll=pairs)
-    work[tiles] = middle
-    work[tiles + 1] = live
-    record = pltpu.make_async_copy(work, work_ref, sems.at[9])
-    record.start()
-    find(pairs)
+        return carry
+
+    lax.fori_loop(0, pairs, find, 0, unroll=pairs)
+    find(pairs, 0)
     lane = lanes(width)
     mine = picked[pairs].astype(bf16)
     for g in range(pairs):
@@ -171,25 +144,22 @@
         part[:, 2 * share + 2 * edge : 2 * share + 3 * edge] = block
     for move in moves:
         move.wait()
-    record.wait()
-
-
-def pick(rows, hub_ids, feats, cotangent, w_self, w_neigh, bias, dst, src, count, peers):
+
+
+def pick(rows, hub_ids, feats, cotangent, w_self, w_neigh, bias, peers):
     width, nodes = feats.shape
     domains, slots = rows.shape
     groups = domains // 2 + 1
-    tiles = dst.shape[0]
     part = jax.ShapeDtypeStruct((width, 2 * nodes // peers + 3 * edge), bf16)
     return pl.pallas_call(
         pick_kernel,
         out_shape=(
             jax.ShapeDtypeStruct((domains, 2 * width, edge), bf16),
             jax.ShapeDtypeStruct((groups, edge), jnp.int32),
-            jax.ShapeDtypeStruct((tiles + edge,), jnp.int32),
         )
         + (part,) * peers,
-        in_specs=[hbm] * 10,
-        out_specs=(vmem,) * (3 + peers),
+        in_specs=[hbm] * 7,
+        out_specs=(vmem,) * (2 + peers),
         scratch_shapes=[
             pltpu.VMEM((width, nodes), bf16),
             pltpu.VMEM((edge,), jnp.int32),
@@ -199,19 +169,12 @@
             pltpu.VMEM((width, edge), bf16),
             pltpu.VMEM((width, edge), bf16),
             pltpu.VMEM((width,), f32),
-            pltpu.SMEM((tiles,), jnp.int32),
-            pltpu.SMEM((tiles,), jnp.int32),
-            pltpu.SMEM((1,), jnp.int32),
-            pltpu.SMEM((tiles + edge,), jnp.int32),
-            pltpu.SemaphoreType.DMA((10,)),
+            pltpu.SemaphoreType.DMA((7,)),
             pltpu.SemaphoreType.DMA((2 * peers,)),
         ],
         compiler_params=params(32),
         name="pick",
-    )(
-        *far_off(rows, hub_ids, feats, cotangent, w_self, w_neigh, bias, dst, src),
-        count,
-    )
+    )(*far_off(rows, hub_ids, feats, cotangent, w_self, w_neigh, bias))
 
 
 def products_of(lefts, tiles, turned):
@@ -337,77 +300,31 @@
     )(*far_off(dst, src), count, *far_off(vals, feats), recv)
 
 
-def fetch(work, vals_ref, held, sems, start, stop):
-    def some(k, carry):
-        for i in range(group):
-            tile = work[jnp.minimum(start + k * group + i, stop - 1)] & 511
-            pltpu.make_async_copy(vals_ref.at[tile], held.at[k * group + i], sems.at[k]).start()
-        return carry
-
-    lax.fori_loop(0, (stop - start + group - 1) // group, some, 0)
-
-
-def fetched(vals_ref, held, sems, k):
-    pltpu.make_async_copy(
-        vals_ref.at[pl.ds(0, group)], held.at[pl.ds(k * group, group)], sems.at[k]
-    ).wait()
-
-
-def visit(work, held, ready, table, total, start, stop, turned):
-    spare = total.shape[0] - 1
-
-    def some(k, carry):
-        slot = k * group
-        first = start + slot
-        lefts, tiles, places = [], [], []
-        for i in range(group):
-            code = work[jnp.minimum(first + i, stop - 1)]
-            target = (code >> 9) & 511
-            source = code >> 18
-            lefts.append(table[source if turned else target])
-            places.append(jnp.where(first + i < stop, target if turned else source, spare))
-        ready(k)
-        for i in range(group):
-            tiles.append(held[slot + i])
-        for place, product in zip(places, products_of(lefts, tiles, turned)):
-            total[place] += product
-        return carry
-
-    lax.fori_loop(0, (stop - start + group - 1) // group, some, 0)
-
-
-def fill_blocks(near_ref, blocks):
-    own = blocks.shape[0]
-    per = own // near_ref.shape[0]
-    for b in range(own):
-        col = (b % per) * edge
-        blocks[b] = near_ref[b // per, :, col : col + edge]
-
-
-def away_kernel(
-    work, near_ref, vals_ref, out_ref, blocks, total, held, tile_sems
+def spread_kernel(
+    dst_ref, src_ref, count_ref, vals_ref, near_ref, out_ref, base_ref, blocks, total, *scratch
 ):
     peers, width, _ = near_ref.shape
     own = blocks.shape[0]
-    share = own // peers * edge
+    per = own // peers
+    share = per * edge
     domains = out_ref.shape[0]
     far = own + domains // 2
-    tiles = vals_ref.shape[0]
-    middle, live = work[tiles], work[tiles + 1]
-    fetch(work, vals_ref, held, tile_sems, middle, live)
-    fill_blocks(near_ref, blocks)
-    total[...] = jnp.zeros_like(total)
 
     def summed(place):
         start = share + place * edge
         return jnp.sum(near_ref[:, :, start : start + edge].astype(f32), axis=0)
 
+    def prepare():
+        for b in range(own):
+            col = (b % per) * edge
+            blocks[b] = near_ref[b // per, :, col : col + edge]
+        total[...] = jnp.zeros_like(total)
+
+    walk_tiles((dst_ref, src_ref, count_ref, vals_ref), scratch, prepare, blocks, total, False)
     grad_self = summed(0).astype(bf16)
     grad_neigh = summed(1).astype(bf16)
     grad_bias = column_block(jnp.sum(summed(2), axis=1, keepdims=True))
     grad_bias = pltpu.roll(grad_bias, edge // 2, 1)
-    ready = functools.partial(fetched, vals_ref, held, tile_sems)
-    visit(work, held, ready, blocks, total, middle, live, False)
     lane = lanes(width)
     for g in range(domains // 2):
         here = total[own + g]
@@ -418,35 +335,32 @@
             out_ref[q, width : 2 * width] = jnp.where(lane < edge // 2, mine, grad_bias).astype(bf16)
             out_ref[q, 2 * width : 3 * width] = grad_self
             out_ref[q, 3 * width : 4 * width] = grad_neigh
-
-
-def away(work, near, vals, domains, nodes):
+    for b in range(own):
+        base_ref[:, b * edge : (b + 1) * edge] = total[b]
+
+
+def spread(dst, src, count, vals, near, domains, nodes):
     _, width, _ = near.shape
-    tiles = vals.shape[0]
     own = nodes // edge
     return pl.pallas_call(
-        away_kernel,
-        out_shape=jax.ShapeDtypeStruct((domains, 4 * width, edge), bf16),
-        in_specs=[smem, vmem, hbm],
-        out_specs=vmem,
+        spread_kernel,
+        out_shape=(
+            jax.ShapeDtypeStruct((domains, 4 * width, edge), bf16),
+            jax.ShapeDtypeStruct((width, nodes), f32),
+        ),
+        in_specs=[hbm] * 4 + [vmem],
+        out_specs=(vmem, vmem),
         scratch_shapes=[
             pltpu.VMEM((own, width, edge), bf16),
             pltpu.VMEM((own + domains // 2 + domains + 1, width, edge), f32),
-            pltpu.VMEM((tiles, edge, edge), bf16),
-            pltpu.SemaphoreType.DMA((tiles // group,)),
-        ],
+        ]
+        + tile_scratch(vals.shape[0]),
         compiler_params=params(32),
-        name="away",
-    )(work, near, *far_off(vals))
-
-
-def home_kernel(work, near_ref, vals_ref, index, out_ref, hots, blocks, total, held, tile_sems):
-    own = blocks.shape[0]
-    tiles = vals_ref.shape[0]
-    stop = work[tiles]
-    fetch(work, vals_ref, held, tile_sems, 0, stop)
-    fill_blocks(near_ref, blocks)
-    total[...] = jnp.zeros_like(total)
+        name="spread",
+    )(*far_off(dst, src), count, *far_off(vals), near)
+
+
+def hot_kernel(index, hots):
     sub = lax.broadcasted_iota(jnp.int32, (span, edge), 0)
     groups = index.shape[0]
     for g in range(groups):
@@ -454,33 +368,17 @@
         hots[:, g * edge : (g + 1) * edge] = hot
     for g in range(groups, groups + 2):
         hots[:, g * edge : (g + 1) * edge] = hot
-    ready = functools.partial(fetched, vals_ref, held, tile_sems)
-    visit(work, held, ready, blocks, total, 0, stop, False)
-    for b in range(own):
-        out_ref[:, b * edge : (b + 1) * edge] = total[b]
-
-
-def home(work, near, vals, index, nodes):
-    _, width, _ = near.shape
-    tiles = vals.shape[0]
-    own = nodes // edge
+
+
+def hot_columns(index):
     return pl.pallas_call(
-        home_kernel,
-        out_shape=(
-            jax.ShapeDtypeStruct((width, nodes), f32),
-            jax.ShapeDtypeStruct((span, (index.shape[0] + 2) * edge), bf16),
-        ),
-        in_specs=[smem, vmem, hbm, vmem],
-        out_specs=(vmem, vmem),
-        scratch_shapes=[
-            pltpu.VMEM((own, width, edge), bf16),
-            pltpu.VMEM((own + 1, width, edge), f32),
-            pltpu.VMEM((tiles, edge, edge), bf16),
-            pltpu.SemaphoreType.DMA((tiles // group,)),
-        ],
-        compiler_params=params(32),
-        name="home",
-    )(work, near, *far_off(vals), index)
+        hot_kernel,
+        out_shape=jax.ShapeDtypeStruct((span, (index.shape[0] + 2) * edge), bf16),
+        in_specs=[vmem],
+        out_specs=vmem,
+        compiler_params=params(16),
+        name="hot_columns",
+    )(index)
 
 
 def layer_kernel(agg_ref, *rest):
@@ -653,7 +551,7 @@
     nodes = feats.shape[1]
     domains = lax.axis_size("dom")
     peers = lax.axis_size("feat")
-    picked, index, work, *parts = pick(
+    picked, index, *parts = pick(
         send_rows[0],
         hub_ids,
         feats,
@@ -661,9 +559,6 @@
         w_self,
         w_neigh,
         bias,
-        tile_dst,
-        tile_src,
-        tile_count,
         peers,
     )
     recv = swap(picked, "dom")
@@ -673,11 +568,11 @@
     agg = swap(agg, "feat")
     near, *lates = layer(agg, parts)
     near = swap(near, "feat")
-    back = away(work, near, tile_vals, domains, nodes)
-    back, lates = lax.optimization_barrier((back, lates))
+    back, base = spread(tile_dst, tile_src, tile_count, tile_vals, near, domains, nodes)
+    back, lates, index = lax.optimization_barrier((back, lates, index))
     back = swap(back, "dom")
     lates = trade(lates, "feat")
-    base, hots = home(work, near, tile_vals, index, nodes)
+    hots = hot_columns(index)
     scale = 1.0 / math.sqrt(nodes * domains)
     return settle(index, hots, back, base, lates, scale)
 

time: 89.9 us -> 86.6 us (0.963)
  Pallas kernels: 18.4 us -> 13.9 us
  waiting for transfers between devices: 10.3 us -> 12.5 us
    pallas_call x2, Pallas kernels: 6.86 us -> 4.02 us  [the longest x1 3.77 us: spread(): pl.pallas_call(spread_kernel, out_shape=(jax.ShapeDtypeStruct((domains, 4...]
    ppermute x14, waiting for transfers between devices: 0.66 us -> 3.46 us  [trade(): lax.ppermute(part, axis, [(i, i ^ k) for i in range(peers)])]
    pallas_call x1, Pallas kernels: 5.74 us -> 3.56 us  [pick(): pl.pallas_call(pick_kernel, out_shape=(jax.ShapeDtypeStruct((domains, 2 *...]
  transfers between devices with their start and end apart: 16 -> 16, of which waited for: 3 -> 5; matrix products, arithmetic and copies ran while one was open for 0% -> 0% of each run, Pallas kernels for 7% -> 5%
where the time goes in v2:
time: 86.6 us; the launch traced here: 86.5 us
  starting transfers between devices  36.1 us (42%)
  blocking collectives  22.6 us (26%)
  Pallas kernels  13.9 us (16%)
  waiting for transfers between devices  12.5 us (14%)
  between operations  1.41 us (2%)
    all_to_all x2, blocking collectives, swap(): return lax.all_to_all(values, axis, split_axis=0, concat_axis=0, tiled=True)  22.6 us
    all_to_all x2, starting transfers between devices, swap(): return lax.all_to_all(values, axis, split_axis=0, concat_axis=0, tiled=True)  19.7 us
    ppermute x14, starting transfers between devices, trade(): lax.ppermute(part, axis, [(i, i ^ k) for i in range(peers)])  16.4 us
    all_to_all x2, waiting for transfers between devices, swap(): return lax.all_to_all(values, axis, split_axis=0, concat_axis=0, tiled=True)  9.03 us
    pallas_call x1, Pallas kernels, gather(): pl.pallas_call(gather_kernel, out_shape=jax.ShapeDtypeStruct((peers, widt...  3.78 us
    pallas_call x1, Pallas kernels, spread(): pl.pallas_call(spread_kernel, out_shape=(jax.ShapeDtypeStruct((domains, 4...  3.77 us
    pallas_call x1, Pallas kernels, pick(): pl.pallas_call(pick_kernel, out_shape=(jax.ShapeDtypeStruct((domains, 2 *...  3.56 us
    ppermute x14, waiting for transfers between devices, trade(): lax.ppermute(part, axis, [(i, i ^ k) for i in range(peers)])  3.46 us
  transfers between devices with their start and end apart: 16, of which 5 were waited for; matrix products, arithmetic and copies ran while one was open for 0% of the time, Pallas kernels for 5%

profile of v2, /device:TPU:32, one launch (start us, length us, event | category | flops | bytes accessed | tf_op | source)
XLA Modules:
  0.0 86.5 jit_solution(214633312985192141)
XLA Ops:
  0.6 3.6 %pick.1 = (bf16[32,32,128]{2,1,0:T(8,128)(2,1)}, s32[17,128]{1,0:T(8,128)S(1)}, bf16[16,2432]{1,0:T(8,128)(2,1)S(1)}, bf16[16,2432]{1,0:T(8,128)(2,1)S(1)}, bf16...) custom-call(s32[32,64]{1,0:T(8,128)} %bitcast.1, ...), custom_call_target="tpu_custom_call" | custom-call | tf_op jit(solution)/shard_map/pick/pallas_call | solution.py:154
  4.2 11.4 %all-to-all-start = ((bf16[32,32,128]{2,1,0:T(8,128)(2,1)}), bf16[32,32,128]{2,1,0:T(8,128)(2,1)S(1)}, u32[]{:S(2)}, u32[]{:S(2)}) async-start(bf16[32,32,128]{2,1,0:T(8,128)(2,1)} %get-tuple-element.45), calls=%async_computation | async-start | bytes 524288 | tf_op jit(solution)/shard_map/all_to_all | solution.py:527
  15.6 0.1 collective-permute-start
  15.7 1.6 %collective-permute-start.1 = (bf16[16,2432]{1,0:T(8,128)(2,1)S(1)}, bf16[16,2432]{1,0:T(8,128)(2,1)S(1)}, u32[]{:S(2)}, u32[]{:S(2)}) collective-permute-start(bf16[16,2432]{1,0:T(8,128)(2,1)S(1)} %get-tuple-element.48), channel_id=1, source_target_pairs={{0,2},{1,3},{2,0},{3,1},{4,6},{5,7},{6,4},{7,5},{8,10},{9,11},{10,... | collective-permute-start | bytes 233480 | tf_op jit(solution)/shard_map/ppermute | solution.py:533
  17.3 0.3 collective-permute-start.2
  17.5 3.0 %collective-permute-start.3 = (bf16[16,2432]{1,0:T(8,128)(2,1)S(1)}, bf16[16,2432]{1,0:T(8,128)(2,1)S(1)}, u32[]{:S(2)}, u32[]{:S(2)}) collective-permute-start(bf16[16,2432]{1,0:T(8,128)(2,1)S(1)} %get-tuple-element.50), channel_id=1, source_target_pairs={{0,4},{1,5},{2,6},{3,7},{4,0},{5,1},{6,2},{7,3},{8,12},{9,13},{10,... | collective-permute-start | bytes 233480 | tf_op jit(solution)/shard_map/ppermute | solution.py:533
  20.6 0.2 collective-permute-start.4
  20.8 0.0 collective-permute-done.rest_1_
  20.8 2.8 %collective-permute-start.5 = (bf16[16,2432]{1,0:T(8,128)(2,1)S(1)}, bf16[16,2432]{1,0:T(8,128)(2,1)S(1)}, u32[]{:S(2)}, u32[]{:S(2)}) collective-permute-start(bf16[16,2432]{1,0:T(8,128)(2,1)S(1)} %get-tuple-element.52), channel_id=1, source_target_pairs={{0,6},{1,7},{2,4},{3,5},{4,2},{5,3},{6,0},{7,1},{8,14},{9,15},{10,... | collective-permute-start | bytes 233480 | tf_op jit(solution)/shard_map/ppermute | solution.py:533
  23.5 0.0 collective-permute-done.1.rest_2_
  23.5 0.2 collective-permute-start.6
  24.4 3.4 %all-to-all-done.recv_ref = bf16[32,32,128]{2,1,0:T(8,128)(2,1)S(1)} async-done(((bf16[32,32,128]{2,1,0:T(8,128)(2,1)}), bf16[32,32,128]{2,1,0:T(8,128)(2,1)S(1)}, u32[]{:S(2)}, u32[]{:S(2)}) %all-to-all-start) | async-done | bytes 262176 | tf_op jit(solution)/shard_map/all_to_all | solution.py:527
  27.9 3.8 %gather.1 = bf16[8,16,1024]{2,1,0:T(8,128)(2,1)S(1)} custom-call(s32[320]{0:T(512)} %dst_ref.3, s32[320]{0:T(512)} %src_ref.3, s32[1]{0:T(128)S(6)} %copy.16.count_ref, bf16[320,128,128]{2,1,0:T(8,128)(2,1)} %vals_ref.3, bf16[16,8192]{1,0:T(8,128)(2,1)} %feats_ref.3, bf16[32,32,128]{2,1,0:T(8,128)(2,1)S(1)} %all-to-all-done.recv_ref), custom_call_target="tpu_custom_call" | custom-call | tf_op jit(solution)/shard_map/gather/pallas_call | solution.py:286
  31.6 0.0 collective-permute-done.2.rest_3_
  31.7 0.0 collective-permute-done.3.rest_4_
  31.7 0.0 collective-permute-done.4.rest_5_
  31.7 0.0 collective-permute-done.5.rest_6_
  31.7 0.0 collective-permute-done.6.rest_7_
  31.7 11.6 %all_to_all.20.agg_ref = bf16[8,16,1024]{2,1,0:T(8,128)(2,1)S(1)} all-to-all(bf16[8,16,1024]{2,1,0:T(8,128)(2,1)S(1)} %gather.1), channel_id=1, replica_groups=mesh['dom'=32,'feat'=8] {'feat'}, dimensions={0} | all-to-all | bytes 524288 | tf_op jit(solution)/shard_map/all_to_all | solution.py:527
  43.3 0.9 %layer.1 = (bf16[8,16,1408]{2,1,0:T(8,128)(2,1)S(1)}, bf16[16,2048]{1,0:T(8,128)(2,1)S(1)}, bf16[16,2048]{1,0:T(8,128)(2,1)S(1)}, bf16[16,2048]{1,0:T(8,128)(2,1...) custom-call(bf16[8,16,1024]{2,1,0:T(8,128)(2,1)S(1)} %all_to_all.20., ...), custom_call_target="tpu_custom_call" | custom-call | tf_op jit(solution)/shard_map/layer/pallas_call | solution.py:432
  44.2 11.0 %all_to_all.21.near_ref = bf16[8,16,1408]{2,1,0:T(8,128)(2,1)S(1)} all-to-all(bf16[8,16,1408]{2,1,0:T(8,128)(2,1)S(1)} %get-tuple-element.63), channel_id=1, replica_groups=mesh['dom'=32,'feat'=8] {'feat'}, dimensions={0} | all-to-all | bytes 720896 | tf_op jit(solution)/shard_map/all_to_all | solution.py:527
  55.2 3.8 %spread.1 = (bf16[32,64,128]{2,1,0:T(8,128)(2,1)}, f32[16,8192]{1,0:T(8,128)S(1)}) custom-call(s32[320]{0:T(512)} %dst_ref.3, s32[320]{0:T(512)} %src_ref.3, s32[1]{0:T(128)S(6)} %copy.16.count_ref, bf16[320,128,128]{2,1,0:T(8,128)(2,1)} %vals_ref.3, bf16[8,16,1408]{2,1,0:T(8,128)(2,1)S(1)} %all_to_all.21.near_ref), custom_call_target="tpu_custom_call" | custom-call | tf_op jit(solution)/shard_map/spread/pallas_call | solution.py:345
  59.0 8.4 %all-to-all-start.3 = ((bf16[32,64,128]{2,1,0:T(8,128)(2,1)}), bf16[32,64,128]{2,1,0:T(8,128)(2,1)S(1)}, u32[]{:S(2)}, u32[]{:S(2)}) async-start(bf16[32,64,128]{2,1,0:T(8,128)(2,1)} %get-tuple-element.75), calls=%async_computation.3 | async-start | bytes 1048576 | tf_op jit(solution)/shard_map/all_to_all | solution.py:527
  67.4 0.1 collective-permute-start.7
  67.5 0.7 collective-permute-start.8
  68.1 1.2 %collective-permute-start.9 = (bf16[16,2048]{1,0:T(8,128)(2,1)S(1)}, bf16[16,2048]{1,0:T(8,128)(2,1)S(1)}, u32[]{:S(2)}, u32[]{:S(2)}) collective-permute-start(bf16[16,2048]{1,0:T(8,128)(2,1)S(1)} %get-tuple-element.80), channel_id=1, source_target_pairs={{0,3},{1,2},{2,1},{3,0},{4,7},{5,6},{6,5},{7,4},{8,11},{9,10},{10,... | collective-permute-start | bytes 196616 | tf_op jit(solution)/shard_map/ppermute | solution.py:533
  69.3 0.9 %collective-permute-start.10 = (bf16[16,2048]{1,0:T(8,128)(2,1)S(1)}, bf16[16,2048]{1,0:T(8,128)(2,1)S(1)}, u32[]{:S(2)}, u32[]{:S(2)}) collective-permute-start(bf16[16,2048]{1,0:T(8,128)(2,1)S(1)} %get-tuple-element.81), channel_id=1, source_target_pairs={{0,4},{1,5},{2,6},{3,7},{4,0},{5,1},{6,2},{7,3},{8,12},{9,13},{10,... | collective-permute-start | bytes 196616 | tf_op jit(solution)/shard_map/ppermute | solution.py:533
  70.3 2.3 %collective-permute-start.11 = (bf16[16,2048]{1,0:T(8,128)(2,1)S(1)}, bf16[16,2048]{1,0:T(8,128)(2,1)S(1)}, u32[]{:S(2)}, u32[]{:S(2)}) collective-permute-start(bf16[16,2048]{1,0:T(8,128)(2,1)S(1)} %get-tuple-element.82), channel_id=1, source_target_pairs={{0,5},{1,4},{2,7},{3,6},{4,1},{5,0},{6,3},{7,2},{8,13},{9,12},{10,... | collective-permute-start | bytes 196616 | tf_op jit(solution)/shard_map/ppermute | solution.py:533
  72.5 0.0 collective-permute-done.7.rest_1_
  72.6 1.2 %collective-permute-start.12 = (bf16[16,2048]{1,0:T(8,128)(2,1)S(1)}, bf16[16,2048]{1,0:T(8,128)(2,1)S(1)}, u32[]{:S(2)}, u32[]{:S(2)}) collective-permute-start(bf16[16,2048]{1,0:T(8,128)(2,1)S(1)} %get-tuple-element.83), channel_id=1, source_target_pairs={{0,6},{1,7},{2,4},{3,5},{4,2},{5,3},{6,0},{7,1},{8,14},{9,15},{10,... | collective-permute-start | bytes 196616 | tf_op jit(solution)/shard_map/ppermute | solution.py:533
  73.7 0.0 collective-permute-done.8.rest_2_
  73.7 1.8 %collective-permute-start.13 = (bf16[16,2048]{1,0:T(8,128)(2,1)S(1)}, bf16[16,2048]{1,0:T(8,128)(2,1)S(1)}, u32[]{:S(2)}, u32[]{:S(2)}) collective-permute-start(bf16[16,2048]{1,0:T(8,128)(2,1)S(1)} %get-tuple-element.84), channel_id=1, source_target_pairs={{0,7},{1,6},{2,5},{3,4},{4,3},{5,2},{6,1},{7,0},{8,15},{9,14},{10,... | collective-permute-start | bytes 196616 | tf_op jit(solution)/shard_map/ppermute | solution.py:533
  75.6 0.2 hot_columns.1.hots
  75.8 0.0 collective-permute-done.9.rest_3_
  75.8 0.0 collective-permute-done.10.rest_4_
  75.8 0.6 collective-permute-done.11.rest_5_
  76.4 2.1 %collective-permute-done.12.rest_6_ = bf16[16,2048]{1,0:T(8,128)(2,1)S(1)} collective-permute-done((bf16[16,2048]{1,0:T(8,128)(2,1)S(1)}, bf16[16,2048]{1,0:T(8,128)(2,1)S(1)}, u32[]{:S(2)}, u32[]{:S(2)}) %collective-permute-start.12) | collective-permute-done | bytes 65568 | tf_op jit(solution)/shard_map/ppermute | solution.py:533
  78.5 0.7 collective-permute-done.13.rest_7_
  79.3 5.6 %all-to-all-done.3.recv_ref = bf16[32,64,128]{2,1,0:T(8,128)(2,1)S(1)} async-done(((bf16[32,64,128]{2,1,0:T(8,128)(2,1)}), bf16[32,64,128]{2,1,0:T(8,128)(2,1)S(1)}, u32[]{:S(2)}, u32[]{:S(2)}) %all-to-all-start.3) | async-done | bytes 524320 | tf_op jit(solution)/shard_map/all_to_all | solution.py:527
  84.9 1.7 %settle.1 = (bf16[16,8192]{1,0:T(8,128)(2,1)}, bf16[16,8192]{1,0:T(8,128)(2,1)}, f32[16,128]{1,0:T(8,128)}, f32[16,128]{1,0:T(8,128)}, f32[16]{0:T(128)}) custom-call(s32[17,128]{1,0:T(8,128)S(1)} %get-tuple-element.74.index, bf16[256,2432]{1,0:T(8,128)(2,1)S(1)} %hot_columns.1.hots, bf16[32,64,128]{2,1,0:T(8,128)(2,1)S(1)} %all-to-all-done.3.recv_ref, ...), custom_call_target="tpu_custom_call" | custom-call | tf_op jit(solution)/shard_map/settle/pallas_call | solution.py:506
Async XLA Ops:
  4.2 23.7 %all-to-all-start = ((bf16[32,32,128]{2,1,0:T(8,128)(2,1)}), bf16[32,32,128]{2,1,0:T(8,128)(2,1)S(1)}, u32[]{:S(2)}, u32[]{:S(2)}) async-start(bf16[32,32,128]{2,1,0:T(8,128)(2,1)} %get-tuple-element.45), calls=%async_computation | async-start | bytes 524288 | tf_op jit(solution)/shard_map/all_to_all | solution.py:527
  15.6 5.2 %collective-permute-start = (bf16[16,2432]{1,0:T(8,128)(2,1)S(1)}, bf16[16,2432]{1,0:T(8,128)(2,1)S(1)}, u32[]{:S(2)}, u32[]{:S(2)}) collective-permute-start(bf16[16,2432]{1,0:T(8,128)(2,1)S(1)} %get-tuple-element.47), channel_id=1, source_target_pairs={{0,1},{1,0},{2,3},{3,2},{4,5},{5,4},{6,7},{7,6},{8,9},{9,8},{10,11... | collective-permute-start | bytes 233480 | tf_op jit(solution)/shard_map/ppermute | solution.py:533
  15.7 7.9 %collective-permute-start.1 = (bf16[16,2432]{1,0:T(8,128)(2,1)S(1)}, bf16[16,2432]{1,0:T(8,128)(2,1)S(1)}, u32[]{:S(2)}, u32[]{:S(2)}) collective-permute-start(bf16[16,2432]{1,0:T(8,128)(2,1)S(1)} %get-tuple-element.48), channel_id=1, source_target_pairs={{0,2},{1,3},{2,0},{3,1},{4,6},{5,7},{6,4},{7,5},{8,10},{9,11},{10,... | collective-permute-start | bytes 233480 | tf_op jit(solution)/shard_map/ppermute | solution.py:533
  17.3 14.4 %collective-permute-start.2 = (bf16[16,2432]{1,0:T(8,128)(2,1)S(1)}, bf16[16,2432]{1,0:T(8,128)(2,1)S(1)}, u32[]{:S(2)}, u32[]{:S(2)}) collective-permute-start(bf16[16,2432]{1,0:T(8,128)(2,1)S(1)} %get-tuple-element.49), channel_id=1, source_target_pairs={{0,3},{1,2},{2,1},{3,0},{4,7},{5,6},{6,5},{7,4},{8,11},{9,10},{10,... | collective-permute-start | bytes 233480 | tf_op jit(solution)/shard_map/ppermute | solution.py:533
  17.5 14.1 %collective-permute-start.3 = (bf16[16,2432]{1,0:T(8,128)(2,1)S(1)}, bf16[16,2432]{1,0:T(8,128)(2,1)S(1)}, u32[]{:S(2)}, u32[]{:S(2)}) collective-permute-start(bf16[16,2432]{1,0:T(8,128)(2,1)S(1)} %get-tuple-element.50), channel_id=1, source_target_pairs={{0,4},{1,5},{2,6},{3,7},{4,0},{5,1},{6,2},{7,3},{8,12},{9,13},{10,... | collective-permute-start | bytes 233480 | tf_op jit(solution)/shard_map/ppermute | solution.py:533
  20.6 11.1 %collective-permute-start.4 = (bf16[16,2432]{1,0:T(8,128)(2,1)S(1)}, bf16[16,2432]{1,0:T(8,128)(2,1)S(1)}, u32[]{:S(2)}, u32[]{:S(2)}) collective-permute-start(bf16[16,2432]{1,0:T(8,128)(2,1)S(1)} %get-tuple-element.51), channel_id=1, source_target_pairs={{0,5},{1,4},{2,7},{3,6},{4,1},{5,0},{6,3},{7,2},{8,13},{9,12},{10,... | collective-permute-start | bytes 233480 | tf_op jit(solution)/shard_map/ppermute | solution.py:533
  20.8 10.9 %collective-permute-start.5 = (bf16[16,2432]{1,0:T(8,128)(2,1)S(1)}, bf16[16,2432]{1,0:T(8,128)(2,1)S(1)}, u32[]{:S(2)}, u32[]{:S(2)}) collective-permute-start(bf16[16,2432]{1,0:T(8,128)(2,1)S(1)} %get-tuple-element.52), channel_id=1, source_target_pairs={{0,6},{1,7},{2,4},{3,5},{4,2},{5,3},{6,0},{7,1},{8,14},{9,15},{10,... | collective-permute-start | bytes 233480 | tf_op jit(solution)/shard_map/ppermute | solution.py:533
  23.5 8.2 %collective-permute-start.6 = (bf16[16,2432]{1,0:T(8,128)(2,1)S(1)}, bf16[16,2432]{1,0:T(8,128)(2,1)S(1)}, u32[]{:S(2)}, u32[]{:S(2)}) collective-permute-start(bf16[16,2432]{1,0:T(8,128)(2,1)S(1)} %get-tuple-element.53), channel_id=1, source_target_pairs={{0,7},{1,6},{2,5},{3,4},{4,3},{5,2},{6,1},{7,0},{8,15},{9,14},{10,... | collective-permute-start | bytes 233480 | tf_op jit(solution)/shard_map/ppermute | solution.py:533
  59.0 25.9 %all-to-all-start.3 = ((bf16[32,64,128]{2,1,0:T(8,128)(2,1)}), bf16[32,64,128]{2,1,0:T(8,128)(2,1)S(1)}, u32[]{:S(2)}, u32[]{:S(2)}) async-start(bf16[32,64,128]{2,1,0:T(8,128)(2,1)} %get-tuple-element.75), calls=%async_computation.3 | async-start | bytes 1048576 | tf_op jit(solution)/shard_map/all_to_all | solution.py:527
  67.4 5.2 %collective-permute-start.7 = (bf16[16,2048]{1,0:T(8,128)(2,1)S(1)}, bf16[16,2048]{1,0:T(8,128)(2,1)S(1)}, u32[]{:S(2)}, u32[]{:S(2)}) collective-permute-start(bf16[16,2048]{1,0:T(8,128)(2,1)S(1)} %get-tuple-element.78), channel_id=1, source_target_pairs={{0,1},{1,0},{2,3},{3,2},{4,5},{5,4},{6,7},{7,6},{8,9},{9,8},{10,11... | collective-permute-start | bytes 196616 | tf_op jit(solution)/shard_map/ppermute | solution.py:533
  67.5 6.3 %collective-permute-start.8 = (bf16[16,2048]{1,0:T(8,128)(2,1)S(1)}, bf16[16,2048]{1,0:T(8,128)(2,1)S(1)}, u32[]{:S(2)}, u32[]{:S(2)}) collective-permute-start(bf16[16,2048]{1,0:T(8,128)(2,1)S(1)} %get-tuple-element.79), channel_id=1, source_target_pairs={{0,2},{1,3},{2,0},{3,1},{4,6},{5,7},{6,4},{7,5},{8,10},{9,11},{10,... | collective-permute-start | bytes 196616 | tf_op jit(solution)/shard_map/ppermute | solution.py:533
  68.1 7.7 %collective-permute-start.9 = (bf16[16,2048]{1,0:T(8,128)(2,1)S(1)}, bf16[16,2048]{1,0:T(8,128)(2,1)S(1)}, u32[]{:S(2)}, u32[]{:S(2)}) collective-permute-start(bf16[16,2048]{1,0:T(8,128)(2,1)S(1)} %get-tuple-element.80), channel_id=1, source_target_pairs={{0,3},{1,2},{2,1},{3,0},{4,7},{5,6},{6,5},{7,4},{8,11},{9,10},{10,... | collective-permute-start | bytes 196616 | tf_op jit(solution)/shard_map/ppermute | solution.py:533
  69.3 6.5 %collective-permute-start.10 = (bf16[16,2048]{1,0:T(8,128)(2,1)S(1)}, bf16[16,2048]{1,0:T(8,128)(2,1)S(1)}, u32[]{:S(2)}, u32[]{:S(2)}) collective-permute-start(bf16[16,2048]{1,0:T(8,128)(2,1)S(1)} %get-tuple-element.81), channel_id=1, source_target_pairs={{0,4},{1,5},{2,6},{3,7},{4,0},{5,1},{6,2},{7,3},{8,12},{9,13},{10,... | collective-permute-start | bytes 196616 | tf_op jit(solution)/shard_map/ppermute | solution.py:533
  70.3 6.1 %collective-permute-start.11 = (bf16[16,2048]{1,0:T(8,128)(2,1)S(1)}, bf16[16,2048]{1,0:T(8,128)(2,1)S(1)}, u32[]{:S(2)}, u32[]{:S(2)}) collective-permute-start(bf16[16,2048]{1,0:T(8,128)(2,1)S(1)} %get-tuple-element.82), channel_id=1, source_target_pairs={{0,5},{1,4},{2,7},{3,6},{4,1},{5,0},{6,3},{7,2},{8,13},{9,12},{10,... | collective-permute-start | bytes 196616 | tf_op jit(solution)/shard_map/ppermute | solution.py:533
  72.6 6.0 %collective-permute-start.12 = (bf16[16,2048]{1,0:T(8,128)(2,1)S(1)}, bf16[16,2048]{1,0:T(8,128)(2,1)S(1)}, u32[]{:S(2)}, u32[]{:S(2)}) collective-permute-start(bf16[16,2048]{1,0:T(8,128)(2,1)S(1)} %get-tuple-element.83), channel_id=1, source_target_pairs={{0,6},{1,7},{2,4},{3,5},{4,2},{5,3},{6,0},{7,1},{8,14},{9,15},{10,... | collective-permute-start | bytes 196616 | tf_op jit(solution)/shard_map/ppermute | solution.py:533
  73.7 5.5 %collective-permute-start.13 = (bf16[16,2048]{1,0:T(8,128)(2,1)S(1)}, bf16[16,2048]{1,0:T(8,128)(2,1)S(1)}, u32[]{:S(2)}, u32[]{:S(2)}) collective-permute-start(bf16[16,2048]{1,0:T(8,128)(2,1)S(1)} %get-tuple-element.84), channel_id=1, source_target_pairs={{0,7},{1,6},{2,5},{3,4},{4,3},{5,2},{6,1},{7,0},{8,15},{9,14},{10,... | collective-permute-start | bytes 196616 | tf_op jit(solution)/shard_map/ppermute | solution.py:533

commit v3 on v2

--- a/solution.py
+++ b/solution.py
@@ -10,8 +10,8 @@
 
 edge = 128
 span = 256
-group = 32
-sure = 2
+group = 64
+sure = 1
 bf16 = jnp.bfloat16
 f32 = jnp.float32
 vmem = pl.BlockSpec(memory_space=pltpu.VMEM)
@@ -46,6 +46,10 @@
     block = jnp.where(lane == 0, hi.astype(f32), 0.0)
     block = jnp.where(lane == 1, mid.astype(f32), block)
     return jnp.where(lane == 2, lo.astype(f32), block)
+
+
+def ways(peers):
+    return sorted(range(peers), key=lambda k: -k.bit_length())
 
 
 def start_all(pairs, sems):
@@ -89,7 +93,7 @@
     )
     here = lax.axis_index("feat")
     moves = []
-    for k, part in enumerate(parts):
+    for k, part in zip(ways(peers), parts):
         there = pl.ds(pl.multiple_of((here ^ k) * share, share), share)
         moves.append((feats_ref.at[:, there], part.at[:, 0:share]))
         moves.append((cotangent_ref.at[:, there], part.at[:, share : 2 * share]))
@@ -301,7 +305,7 @@
 
 
 def spread_kernel(
-    dst_ref, src_ref, count_ref, vals_ref, near_ref, out_ref, base_ref, blocks, total, *scratch
+    dst_ref, src_ref, count_ref, vals_ref, near_ref, out_ref, base_ref, blocks, total, tail, *scratch
 ):
     peers, width, _ = near_ref.shape
     own = blocks.shape[0]
@@ -319,12 +323,16 @@
             col = (b % per) * edge
             blocks[b] = near_ref[b // per, :, col : col + edge]
         total[...] = jnp.zeros_like(total)
+        grad_self = summed(0).astype(bf16)
+        grad_neigh = summed(1).astype(bf16)
+        grad_bias = column_block(jnp.sum(summed(2), axis=1, keepdims=True))
+        tail[...] = pltpu.roll(grad_bias, edge // 2, 1)
+        for q in range(domains):
+            out_ref[q, 2 * width : 3 * width] = grad_self
+            out_ref[q, 3 * width : 4 * width] = grad_neigh
 
     walk_tiles((dst_ref, src_ref, count_ref, vals_ref), scratch, prepare, blocks, total, False)
-    grad_self = summed(0).astype(bf16)
-    grad_neigh = summed(1).astype(bf16)
-    grad_bias = column_block(jnp.sum(summed(2), axis=1, keepdims=True))
-    grad_bias = pltpu.roll(grad_bias, edge // 2, 1)
+    grad_bias = tail[...]
     lane = lanes(width)
     for g in range(domains // 2):
         here = total[own + g]
@@ -333,8 +341,6 @@
             mine = pltpu.roll(here, edge // 2, 1) if odd else here
             out_ref[q, 0:width] = total[far + q].astype(bf16)
             out_ref[q, width : 2 * width] = jnp.where(lane < edge // 2, mine, grad_bias).astype(bf16)
-            out_ref[q, 2 * width : 3 * width] = grad_self
-            out_ref[q, 3 * width : 4 * width] = grad_neigh
     for b in range(own):
         base_ref[:, b * edge : (b + 1) * edge] = total[b]
 
@@ -353,6 +359,7 @@
         scratch_shapes=[
             pltpu.VMEM((own, width, edge), bf16),
             pltpu.VMEM((own + domains // 2 + domains + 1, width, edge), f32),
+            pltpu.VMEM((width, edge), f32),
         ]
         + tile_scratch(vals.shape[0]),
         compiler_params=params(32),
@@ -387,7 +394,7 @@
     parts, near_ref, lates = rest[:peers], rest[peers], rest[peers + 1 : 2 * peers + 1]
     feats_all, cotangent_all, self_all, neigh_all, bias_all, act, back = rest[2 * peers + 1 :]
     here = lax.axis_index("feat")
-    for k, part in enumerate(parts):
+    for k, part in zip(ways(peers), parts):
         peer = here ^ k
         feats_all[peer] = part[:, 0:share]
         cotangent_all[peer] = part[:, share : 2 * share]
@@ -421,7 +428,7 @@
     for place, piece in enumerate((grad_self.astype(bf16), grad_neigh.astype(bf16), grad_bias)):
         start = share + place * edge
         near_ref[:, :, start : start + edge] = piece.reshape(peers, width, edge)
-    for k, late in enumerate(lates):
+    for k, late in zip(ways(peers), lates):
         peer = here ^ k
         late[:, 0:share] = act[peer]
         late[:, share : 2 * share] = back[peer]
@@ -459,7 +466,7 @@
     count = nodes // span
     pairs = domains // 2
     here = lax.axis_index("feat")
-    for k, late in enumerate(lates):
+    for k, late in zip(ways(peers), lates):
         peer = here ^ k
         act_ref[:, pl.ds(pl.multiple_of(peer * share, share), share)] = late[:, 0:share]
         back[:, pl.ds(pl.multiple_of(peer * share, share), share)] = late[:, share : 2 * share]
@@ -530,8 +537,8 @@
 def trade(parts, axis):
     peers = len(parts)
     return [
-        part if k == 0 else lax.ppermute(part, axis, [(i, i ^ k) for i in range(peers)])
-        for k, part in enumerate(parts)
+        lax.ppermute(part, axis, [(i, i ^ k) for i in range(peers)]) if k else part
+        for k, part in zip(ways(peers), parts)
     ]
 
 

time: 86.6 us -> 87.2 us (level)
  transfers between devices with their start and end apart: 16 -> 16, of which waited for: 5 -> 6; matrix products, arithmetic and copies ran while one was open for 0% -> 0% of each run, Pallas kernels for 5% -> 5%
where the time goes in v3:
time: 87.2 us; the launch traced here: 87.1 us
  starting transfers between devices  36.5 us (42%)
  blocking collectives  22.6 us (26%)
  Pallas kernels  14 us (16%)
  waiting for transfers between devices  12.7 us (15%)
  between operations  1.39 us (2%)
    all_to_all x2, blocking collectives, swap(): return lax.all_to_all(values, axis, split_axis=0, concat_axis=0, tiled=True)  22.6 us
    all_to_all x2, starting transfers between devices, swap(): return lax.all_to_all(values, axis, split_axis=0, concat_axis=0, tiled=True)  20.3 us
    ppermute x14, starting transfers between devices, trade(): lax.ppermute(part, axis, [(i, i ^ k) for i in range(peers)])  16.2 us
    all_to_all x2, waiting for transfers between devices, swap(): return lax.all_to_all(values, axis, split_axis=0, concat_axis=0, tiled=True)  9.84 us
    pallas_call x1, Pallas kernels, spread(): pl.pallas_call(spread_kernel, out_shape=(jax.ShapeDtypeStruct((domains, 4...  3.85 us
    pallas_call x1, Pallas kernels, gather(): pl.pallas_call(gather_kernel, out_shape=jax.ShapeDtypeStruct((peers, widt...  3.74 us
    pallas_call x1, Pallas kernels, pick(): pl.pallas_call(pick_kernel, out_shape=(jax.ShapeDtypeStruct((domains, 2 *...  3.55 us
    ppermute x14, waiting for transfers between devices, trade(): lax.ppermute(part, axis, [(i, i ^ k) for i in range(peers)])  2.87 us
  transfers between devices with their start and end apart: 16, of which 6 were waited for; matrix products, arithmetic and copies ran while one was open for 0% of the time, Pallas kernels for 5%

profile of v3, /device:TPU:32, one launch (start us, length us, event | category | flops | bytes accessed | tf_op | source)
XLA Modules:
  0.0 87.1 jit_solution(8286463108390193759)
XLA Ops:
  0.6 3.6 %pick.1 = (bf16[32,32,128]{2,1,0:T(8,128)(2,1)}, s32[17,128]{1,0:T(8,128)S(1)}, bf16[16,2432]{1,0:T(8,128)(2,1)S(1)}, bf16[16,2432]{1,0:T(8,128)(2,1)S(1)}, bf16...) custom-call(s32[32,64]{1,0:T(8,128)} %bitcast.1, ...), custom_call_target="tpu_custom_call" | custom-call | tf_op jit(solution)/shard_map/pick/pallas_call | solution.py:158
  4.2 11.4 %all-to-all-start = ((bf16[32,32,128]{2,1,0:T(8,128)(2,1)}), bf16[32,32,128]{2,1,0:T(8,128)(2,1)S(1)}, u32[]{:S(2)}, u32[]{:S(2)}) async-start(bf16[32,32,128]{2,1,0:T(8,128)(2,1)} %get-tuple-element.45), calls=%async_computation | async-start | bytes 524288 | tf_op jit(solution)/shard_map/all_to_all | solution.py:534
  15.6 3.1 %collective-permute-start = (bf16[16,2432]{1,0:T(8,128)(2,1)S(1)}, bf16[16,2432]{1,0:T(8,128)(2,1)S(1)}, u32[]{:S(2)}, u32[]{:S(2)}) collective-permute-start(bf16[16,2432]{1,0:T(8,128)(2,1)S(1)} %get-tuple-element.46), channel_id=1, source_target_pairs={{0,4},{1,5},{2,6},{3,7},{4,0},{5,1},{6,2},{7,3},{8,12},{9,13},{10,... | collective-permute-start | bytes 233480 | tf_op jit(solution)/shard_map/ppermute | solution.py:540
  18.7 0.0 collective-permute-start.1
  18.7 1.9 %collective-permute-start.2 = (bf16[16,2432]{1,0:T(8,128)(2,1)S(1)}, bf16[16,2432]{1,0:T(8,128)(2,1)S(1)}, u32[]{:S(2)}, u32[]{:S(2)}) collective-permute-start(bf16[16,2432]{1,0:T(8,128)(2,1)S(1)} %get-tuple-element.48), channel_id=1, source_target_pairs={{0,6},{1,7},{2,4},{3,5},{4,2},{5,3},{6,0},{7,1},{8,14},{9,15},{10,... | collective-permute-start | bytes 233480 | tf_op jit(solution)/shard_map/ppermute | solution.py:540
  20.5 1.3 %collective-permute-start.3 = (bf16[16,2432]{1,0:T(8,128)(2,1)S(1)}, bf16[16,2432]{1,0:T(8,128)(2,1)S(1)}, u32[]{:S(2)}, u32[]{:S(2)}) collective-permute-start(bf16[16,2432]{1,0:T(8,128)(2,1)S(1)} %get-tuple-element.49), channel_id=1, source_target_pairs={{0,7},{1,6},{2,5},{3,4},{4,3},{5,2},{6,1},{7,0},{8,15},{9,14},{10,... | collective-permute-start | bytes 233480 | tf_op jit(solution)/shard_map/ppermute | solution.py:540
  21.9 0.3 collective-permute-start.4
  22.1 0.0 collective-permute-done.rest_0_
  22.1 1.2 %collective-permute-start.5 = (bf16[16,2432]{1,0:T(8,128)(2,1)S(1)}, bf16[16,2432]{1,0:T(8,128)(2,1)S(1)}, u32[]{:S(2)}, u32[]{:S(2)}) collective-permute-start(bf16[16,2432]{1,0:T(8,128)(2,1)S(1)} %get-tuple-element.51), channel_id=1, source_target_pairs={{0,3},{1,2},{2,1},{3,0},{4,7},{5,6},{6,5},{7,4},{8,11},{9,10},{10,... | collective-permute-start | bytes 233480 | tf_op jit(solution)/shard_map/ppermute | solution.py:540
  23.4 0.7 collective-permute-done.1.rest_1_
  24.1 0.0 collective-permute-start.6
  24.8 3.1 %all-to-all-done.recv_ref = bf16[32,32,128]{2,1,0:T(8,128)(2,1)S(1)} async-done(((bf16[32,32,128]{2,1,0:T(8,128)(2,1)}), bf16[32,32,128]{2,1,0:T(8,128)(2,1)S(1)}, u32[]{:S(2)}, u32[]{:S(2)}) %all-to-all-start) | async-done | bytes 262176 | tf_op jit(solution)/shard_map/all_to_all | solution.py:534
  27.9 3.7 %gather.1 = bf16[8,16,1024]{2,1,0:T(8,128)(2,1)S(1)} custom-call(s32[320]{0:T(512)} %dst_ref.3, s32[320]{0:T(512)} %src_ref.3, s32[1]{0:T(128)S(6)} %copy.16.count_ref, bf16[320,128,128]{2,1,0:T(8,128)(2,1)} %vals_ref.3, bf16[16,8192]{1,0:T(8,128)(2,1)} %feats_ref.3, bf16[32,32,128]{2,1,0:T(8,128)(2,1)S(1)} %all-to-all-done.recv_ref), custom_call_target="tpu_custom_call" | custom-call | tf_op jit(solution)/shard_map/gather/pallas_call | solution.py:290
  31.6 0.0 collective-permute-done.2.rest_2_
  31.6 0.0 collective-permute-done.3.rest_3_
  31.6 0.0 collective-permute-done.4.rest_4_
  31.6 0.0 collective-permute-done.5.rest_5_
  31.7 0.0 collective-permute-done.6.rest_6_
  31.7 11.6 %all_to_all.20.agg_ref = bf16[8,16,1024]{2,1,0:T(8,128)(2,1)S(1)} all-to-all(bf16[8,16,1024]{2,1,0:T(8,128)(2,1)S(1)} %gather.1), channel_id=1, replica_groups=mesh['dom'=32,'feat'=8] {'feat'}, dimensions={0} | all-to-all | bytes 524288 | tf_op jit(solution)/shard_map/all_to_all | solution.py:534
  43.3 0.9 %layer.1 = (bf16[8,16,1408]{2,1,0:T(8,128)(2,1)S(1)}, bf16[16,2048]{1,0:T(8,128)(2,1)S(1)}, bf16[16,2048]{1,0:T(8,128)(2,1)S(1)}, bf16[16,2048]{1,0:T(8,128)(2,1...) custom-call(bf16[8,16,1024]{2,1,0:T(8,128)(2,1)S(1)} %all_to_all.20., ...), custom_call_target="tpu_custom_call" | custom-call | tf_op jit(solution)/shard_map/layer/pallas_call | solution.py:439
  44.2 11.0 %all_to_all.21.near_ref = bf16[8,16,1408]{2,1,0:T(8,128)(2,1)S(1)} all-to-all(bf16[8,16,1408]{2,1,0:T(8,128)(2,1)S(1)} %get-tuple-element.63), channel_id=1, replica_groups=mesh['dom'=32,'feat'=8] {'feat'}, dimensions={0} | all-to-all | bytes 720896 | tf_op jit(solution)/shard_map/all_to_all | solution.py:534
  55.2 3.9 %spread.1 = (bf16[32,64,128]{2,1,0:T(8,128)(2,1)}, f32[16,8192]{1,0:T(8,128)S(1)}) custom-call(s32[320]{0:T(512)} %dst_ref.3, s32[320]{0:T(512)} %src_ref.3, s32[1]{0:T(128)S(6)} %copy.16.count_ref, bf16[320,128,128]{2,1,0:T(8,128)(2,1)} %vals_ref.3, bf16[8,16,1408]{2,1,0:T(8,128)(2,1)S(1)} %all_to_all.21.near_ref), custom_call_target="tpu_custom_call" | custom-call | tf_op jit(solution)/shard_map/spread/pallas_call | solution.py:351
  59.0 8.9 %all-to-all-start.3 = ((bf16[32,64,128]{2,1,0:T(8,128)(2,1)}), bf16[32,64,128]{2,1,0:T(8,128)(2,1)S(1)}, u32[]{:S(2)}, u32[]{:S(2)}) async-start(bf16[32,64,128]{2,1,0:T(8,128)(2,1)} %get-tuple-element.75), calls=%async_computation.3 | async-start | bytes 1048576 | tf_op jit(solution)/shard_map/all_to_all | solution.py:534
  67.9 1.0 %collective-permute-start.7 = (bf16[16,2048]{1,0:T(8,128)(2,1)S(1)}, bf16[16,2048]{1,0:T(8,128)(2,1)S(1)}, u32[]{:S(2)}, u32[]{:S(2)}) collective-permute-start(bf16[16,2048]{1,0:T(8,128)(2,1)S(1)} %get-tuple-element.77), channel_id=1, source_target_pairs={{0,4},{1,5},{2,6},{3,7},{4,0},{5,1},{6,2},{7,3},{8,12},{9,13},{10,... | collective-permute-start | bytes 196616 | tf_op jit(solution)/shard_map/ppermute | solution.py:540
  68.9 1.1 %collective-permute-start.8 = (bf16[16,2048]{1,0:T(8,128)(2,1)S(1)}, bf16[16,2048]{1,0:T(8,128)(2,1)S(1)}, u32[]{:S(2)}, u32[]{:S(2)}) collective-permute-start(bf16[16,2048]{1,0:T(8,128)(2,1)S(1)} %get-tuple-element.78), channel_id=1, source_target_pairs={{0,5},{1,4},{2,7},{3,6},{4,1},{5,0},{6,3},{7,2},{8,13},{9,12},{10,... | collective-permute-start | bytes 196616 | tf_op jit(solution)/shard_map/ppermute | solution.py:540
  70.0 1.3 %collective-permute-start.9 = (bf16[16,2048]{1,0:T(8,128)(2,1)S(1)}, bf16[16,2048]{1,0:T(8,128)(2,1)S(1)}, u32[]{:S(2)}, u32[]{:S(2)}) collective-permute-start(bf16[16,2048]{1,0:T(8,128)(2,1)S(1)} %get-tuple-element.79), channel_id=1, source_target_pairs={{0,6},{1,7},{2,4},{3,5},{4,2},{5,3},{6,0},{7,1},{8,14},{9,15},{10,... | collective-permute-start | bytes 196616 | tf_op jit(solution)/shard_map/ppermute | solution.py:540
  71.3 3.0 %collective-permute-start.10 = (bf16[16,2048]{1,0:T(8,128)(2,1)S(1)}, bf16[16,2048]{1,0:T(8,128)(2,1)S(1)}, u32[]{:S(2)}, u32[]{:S(2)}) collective-permute-start(bf16[16,2048]{1,0:T(8,128)(2,1)S(1)} %get-tuple-element.80), channel_id=1, source_target_pairs={{0,7},{1,6},{2,5},{3,4},{4,3},{5,2},{6,1},{7,0},{8,15},{9,14},{10,... | collective-permute-start | bytes 196616 | tf_op jit(solution)/shard_map/ppermute | solution.py:540
  74.3 0.0 collective-permute-start.11
  74.3 0.0 collective-permute-done.7.rest_0_
  74.3 0.4 collective-permute-start.12
  74.7 0.1 collective-permute-done.8.rest_1_
  74.8 1.6 %collective-permute-start.13 = (bf16[16,2048]{1,0:T(8,128)(2,1)S(1)}, bf16[16,2048]{1,0:T(8,128)(2,1)S(1)}, u32[]{:S(2)}, u32[]{:S(2)}) collective-permute-start(bf16[16,2048]{1,0:T(8,128)(2,1)S(1)} %get-tuple-element.83), channel_id=1, source_target_pairs={{0,1},{1,0},{2,3},{3,2},{4,5},{5,4},{6,7},{7,6},{8,9},{9,8},{10,11... | collective-permute-start | bytes 196616 | tf_op jit(solution)/shard_map/ppermute | solution.py:540
  76.4 0.2 hot_columns.1.hots
  76.7 0.0 collective-permute-done.9.rest_2_
  76.7 1.0 %collective-permute-done.10.rest_3_ = bf16[16,2048]{1,0:T(8,128)(2,1)S(1)} collective-permute-done((bf16[16,2048]{1,0:T(8,128)(2,1)S(1)}, bf16[16,2048]{1,0:T(8,128)(2,1)S(1)}, u32[]{:S(2)}, u32[]{:S(2)}) %collective-permute-start.10) | collective-permute-done | bytes 65568 | tf_op jit(solution)/shard_map/ppermute | solution.py:540
  77.6 1.1 %collective-permute-done.11.rest_4_ = bf16[16,2048]{1,0:T(8,128)(2,1)S(1)} collective-permute-done((bf16[16,2048]{1,0:T(8,128)(2,1)S(1)}, bf16[16,2048]{1,0:T(8,128)(2,1)S(1)}, u32[]{:S(2)}, u32[]{:S(2)}) %collective-permute-start.11) | collective-permute-done | bytes 65568 | tf_op jit(solution)/shard_map/ppermute | solution.py:540
  78.7 0.0 collective-permute-done.12.rest_5_
  78.7 0.0 collective-permute-done.13.rest_6_
  78.7 6.7 %all-to-all-done.3.recv_ref = bf16[32,64,128]{2,1,0:T(8,128)(2,1)S(1)} async-done(((bf16[32,64,128]{2,1,0:T(8,128)(2,1)}), bf16[32,64,128]{2,1,0:T(8,128)(2,1)S(1)}, u32[]{:S(2)}, u32[]{:S(2)}) %all-to-all-start.3) | async-done | bytes 524320 | tf_op jit(solution)/shard_map/all_to_all | solution.py:534
  85.4 1.7 %settle.1 = (bf16[16,8192]{1,0:T(8,128)(2,1)}, bf16[16,8192]{1,0:T(8,128)(2,1)}, f32[16,128]{1,0:T(8,128)}, f32[16,128]{1,0:T(8,128)}, f32[16]{0:T(128)}) custom-call(s32[17,128]{1,0:T(8,128)S(1)} %get-tuple-element.74.index, bf16[256,2432]{1,0:T(8,128)(2,1)S(1)} %hot_columns.1.hots, bf16[32,64,128]{2,1,0:T(8,128)(2,1)S(1)} %all-to-all-done.3.recv_ref, ...), custom_call_target="tpu_custom_call" | custom-call | tf_op jit(solution)/shard_map/settle/pallas_call | solution.py:513
Async XLA Ops:
  4.2 23.7 %all-to-all-start = ((bf16[32,32,128]{2,1,0:T(8,128)(2,1)}), bf16[32,32,128]{2,1,0:T(8,128)(2,1)S(1)}, u32[]{:S(2)}, u32[]{:S(2)}) async-start(bf16[32,32,128]{2,1,0:T(8,128)(2,1)} %get-tuple-element.45), calls=%async_computation | async-start | bytes 524288 | tf_op jit(solution)/shard_map/all_to_all | solution.py:534
  15.6 6.6 %collective-permute-start = (bf16[16,2432]{1,0:T(8,128)(2,1)S(1)}, bf16[16,2432]{1,0:T(8,128)(2,1)S(1)}, u32[]{:S(2)}, u32[]{:S(2)}) collective-permute-start(bf16[16,2432]{1,0:T(8,128)(2,1)S(1)} %get-tuple-element.46), channel_id=1, source_target_pairs={{0,4},{1,5},{2,6},{3,7},{4,0},{5,1},{6,2},{7,3},{8,12},{9,13},{10,... | collective-permute-start | bytes 233480 | tf_op jit(solution)/shard_map/ppermute | solution.py:540
  18.7 5.4 %collective-permute-start.1 = (bf16[16,2432]{1,0:T(8,128)(2,1)S(1)}, bf16[16,2432]{1,0:T(8,128)(2,1)S(1)}, u32[]{:S(2)}, u32[]{:S(2)}) collective-permute-start(bf16[16,2432]{1,0:T(8,128)(2,1)S(1)} %get-tuple-element.47), channel_id=1, source_target_pairs={{0,5},{1,4},{2,7},{3,6},{4,1},{5,0},{6,3},{7,2},{8,13},{9,12},{10,... | collective-permute-start | bytes 233480 | tf_op jit(solution)/shard_map/ppermute | solution.py:540
  18.7 12.9 %collective-permute-start.2 = (bf16[16,2432]{1,0:T(8,128)(2,1)S(1)}, bf16[16,2432]{1,0:T(8,128)(2,1)S(1)}, u32[]{:S(2)}, u32[]{:S(2)}) collective-permute-start(bf16[16,2432]{1,0:T(8,128)(2,1)S(1)} %get-tuple-element.48), channel_id=1, source_target_pairs={{0,6},{1,7},{2,4},{3,5},{4,2},{5,3},{6,0},{7,1},{8,14},{9,15},{10,... | collective-permute-start | bytes 233480 | tf_op jit(solution)/shard_map/ppermute | solution.py:540
  20.5 11.1 %collective-permute-start.3 = (bf16[16,2432]{1,0:T(8,128)(2,1)S(1)}, bf16[16,2432]{1,0:T(8,128)(2,1)S(1)}, u32[]{:S(2)}, u32[]{:S(2)}) collective-permute-start(bf16[16,2432]{1,0:T(8,128)(2,1)S(1)} %get-tuple-element.49), channel_id=1, source_target_pairs={{0,7},{1,6},{2,5},{3,4},{4,3},{5,2},{6,1},{7,0},{8,15},{9,14},{10,... | collective-permute-start | bytes 233480 | tf_op jit(solution)/shard_map/ppermute | solution.py:540
  21.9 9.8 %collective-permute-start.4 = (bf16[16,2432]{1,0:T(8,128)(2,1)S(1)}, bf16[16,2432]{1,0:T(8,128)(2,1)S(1)}, u32[]{:S(2)}, u32[]{:S(2)}) collective-permute-start(bf16[16,2432]{1,0:T(8,128)(2,1)S(1)} %get-tuple-element.50), channel_id=1, source_target_pairs={{0,2},{1,3},{2,0},{3,1},{4,6},{5,7},{6,4},{7,5},{8,10},{9,11},{10,... | collective-permute-start | bytes 233480 | tf_op jit(solution)/shard_map/ppermute | solution.py:540
  22.1 9.5 %collective-permute-start.5 = (bf16[16,2432]{1,0:T(8,128)(2,1)S(1)}, bf16[16,2432]{1,0:T(8,128)(2,1)S(1)}, u32[]{:S(2)}, u32[]{:S(2)}) collective-permute-start(bf16[16,2432]{1,0:T(8,128)(2,1)S(1)} %get-tuple-element.51), channel_id=1, source_target_pairs={{0,3},{1,2},{2,1},{3,0},{4,7},{5,6},{6,5},{7,4},{8,11},{9,10},{10,... | collective-permute-start | bytes 233480 | tf_op jit(solution)/shard_map/ppermute | solution.py:540
  24.1 7.6 %collective-permute-start.6 = (bf16[16,2432]{1,0:T(8,128)(2,1)S(1)}, bf16[16,2432]{1,0:T(8,128)(2,1)S(1)}, u32[]{:S(2)}, u32[]{:S(2)}) collective-permute-start(bf16[16,2432]{1,0:T(8,128)(2,1)S(1)} %get-tuple-element.52), channel_id=1, source_target_pairs={{0,1},{1,0},{2,3},{3,2},{4,5},{5,4},{6,7},{7,6},{8,9},{9,8},{10,11... | collective-permute-start | bytes 233480 | tf_op jit(solution)/shard_map/ppermute | solution.py:540
  59.0 26.4 %all-to-all-start.3 = ((bf16[32,64,128]{2,1,0:T(8,128)(2,1)}), bf16[32,64,128]{2,1,0:T(8,128)(2,1)S(1)}, u32[]{:S(2)}, u32[]{:S(2)}) async-start(bf16[32,64,128]{2,1,0:T(8,128)(2,1)} %get-tuple-element.75), calls=%async_computation.3 | async-start | bytes 1048576 | tf_op jit(solution)/shard_map/all_to_all | solution.py:534
  67.9 6.3 %collective-permute-start.7 = (bf16[16,2048]{1,0:T(8,128)(2,1)S(1)}, bf16[16,2048]{1,0:T(8,128)(2,1)S(1)}, u32[]{:S(2)}, u32[]{:S(2)}) collective-permute-start(bf16[16,2048]{1,0:T(8,128)(2,1)S(1)} %get-tuple-element.77), channel_id=1, source_target_pairs={{0,4},{1,5},{2,6},{3,7},{4,0},{5,1},{6,2},{7,3},{8,12},{9,13},{10,... | collective-permute-start | bytes 196616 | tf_op jit(solution)/shard_map/ppermute | solution.py:540
  68.9 5.9 %collective-permute-start.8 = (bf16[16,2048]{1,0:T(8,128)(2,1)S(1)}, bf16[16,2048]{1,0:T(8,128)(2,1)S(1)}, u32[]{:S(2)}, u32[]{:S(2)}) collective-permute-start(bf16[16,2048]{1,0:T(8,128)(2,1)S(1)} %get-tuple-element.78), channel_id=1, source_target_pairs={{0,5},{1,4},{2,7},{3,6},{4,1},{5,0},{6,3},{7,2},{8,13},{9,12},{10,... | collective-permute-start | bytes 196616 | tf_op jit(solution)/shard_map/ppermute | solution.py:540
  70.0 6.7 %collective-permute-start.9 = (bf16[16,2048]{1,0:T(8,128)(2,1)S(1)}, bf16[16,2048]{1,0:T(8,128)(2,1)S(1)}, u32[]{:S(2)}, u32[]{:S(2)}) collective-permute-start(bf16[16,2048]{1,0:T(8,128)(2,1)S(1)} %get-tuple-element.79), channel_id=1, source_target_pairs={{0,6},{1,7},{2,4},{3,5},{4,2},{5,3},{6,0},{7,1},{8,14},{9,15},{10,... | collective-permute-start | bytes 196616 | tf_op jit(solution)/shard_map/ppermute | solution.py:540
  71.3 6.4 %collective-permute-start.10 = (bf16[16,2048]{1,0:T(8,128)(2,1)S(1)}, bf16[16,2048]{1,0:T(8,128)(2,1)S(1)}, u32[]{:S(2)}, u32[]{:S(2)}) collective-permute-start(bf16[16,2048]{1,0:T(8,128)(2,1)S(1)} %get-tuple-element.80), channel_id=1, source_target_pairs={{0,7},{1,6},{2,5},{3,4},{4,3},{5,2},{6,1},{7,0},{8,15},{9,14},{10,... | collective-permute-start | bytes 196616 | tf_op jit(solution)/shard_map/ppermute | solution.py:540
  74.3 4.4 %collective-permute-start.11 = (bf16[16,2048]{1,0:T(8,128)(2,1)S(1)}, bf16[16,2048]{1,0:T(8,128)(2,1)S(1)}, u32[]{:S(2)}, u32[]{:S(2)}) collective-permute-start(bf16[16,2048]{1,0:T(8,128)(2,1)S(1)} %get-tuple-element.81), channel_id=1, source_target_pairs={{0,2},{1,3},{2,0},{3,1},{4,6},{5,7},{6,4},{7,5},{8,10},{9,11},{10,... | collective-permute-start | bytes 196616 | tf_op jit(solution)/shard_map/ppermute | solution.py:540
  74.3 4.4 %collective-permute-start.12 = (bf16[16,2048]{1,0:T(8,128)(2,1)S(1)}, bf16[16,2048]{1,0:T(8,128)(2,1)S(1)}, u32[]{:S(2)}, u32[]{:S(2)}) collective-permute-start(bf16[16,2048]{1,0:T(8,128)(2,1)S(1)} %get-tuple-element.82), channel_id=1, source_target_pairs={{0,3},{1,2},{2,1},{3,0},{4,7},{5,6},{6,5},{7,4},{8,11},{9,10},{10,... | collective-permute-start | bytes 196616 | tf_op jit(solution)/shard_map/ppermute | solution.py:540
  74.8 3.9 %collective-permute-start.13 = (bf16[16,2048]{1,0:T(8,128)(2,1)S(1)}, bf16[16,2048]{1,0:T(8,128)(2,1)S(1)}, u32[]{:S(2)}, u32[]{:S(2)}) collective-permute-start(bf16[16,2048]{1,0:T(8,128)(2,1)S(1)} %get-tuple-element.83), channel_id=1, source_target_pairs={{0,1},{1,0},{2,3},{3,2},{4,5},{5,4},{6,7},{7,6},{8,9},{9,8},{10,11... | collective-permute-start | bytes 196616 | tf_op jit(solution)/shard_map/ppermute | solution.py:540
